TPU v7x, 128 devices: a whole 4x4x4 slice. The times are simulated.
128 devices in a mesh: lon: 16 (over y, z_hi, core), lat: 8 (over x, z_lo).
Axes of the slice: x: 4, y: 4, z: 4 (z_hi: 2, z_lo: 2; z = z_hi * 2 + z_lo), core: 2. Of those that a mesh axis runs over, the one named last changes fastest.
Arguments:
- adjoint_state: float32 [3, 72, 256, 2048], P(None, None, 'lat', 'lon'), may hold values from -6 to 6
- outflow: float32 [4, 72, 256, 2048], P(None, None, 'lat', 'lon'), may hold values from 0 to 0.25
- mix_blocks: float32 [256, 3, 24, 24], P('lat'), may hold values from -1 to 1
- sounding_owner: int32 [524288, 1], P(('lon', 'lat')), may hold values from 0 to 127; in each aligned block of 4096 rows (0 to 4095, 4096 to 8191, ...) at most 64 rows name the same one
- path_column: int32 [524288, 4], P(('lon', 'lat')), may hold values from 0 to 4095
- path_level: int32 [524288, 3], P(('lon', 'lat')), may hold values from 0 to 72
- kernel_weights: float32 [72, 1048576], P(None, ('lon', 'lat')), may hold values from -0.75 to 0.75
Outputs:
- adjoint_final: float32 [3, 72, 256, 2048], P(None, None, 'lat', 'lon')
- slant_sensitivity: float32 [1048576], P(('lon', 'lat'))
Inputs may be any that keep to these rules, and one draw needn't show every extreme that they name: `sounding_owner`: the 4096 soundings of one block name one owner at most 64 times, a bound that some block reaches.
All inputs are finite; a program needn't handle non-finite values.
Results may differ from a plain program's by a relative error of at most 0.0003.
Values sent between devices are 32-bit elements; how exact they have to be, the bound alone decides.
No kernel may reach another device: no remote copies, remote signals or barrier semaphores. Data moves between devices by JAX's collectives and lax.ppermute only.
A program may use at most 192 MiB of HBM per device.

v0:
```python
import jax
import jax.numpy as jnp
from jax import lax
from jax.experimental import pallas as pl
from jax.experimental.pallas import tpu as pltpu
from jax.sharding import PartitionSpec as P

T, L, NB, BL, Y, X = 3, 72, 3, 24, 32, 128
OWN, CAP, SND = 128, 64, 4096
YT = Y // 8
K = 8 * BL
ROWS = 40
GROUPS = SND // 128
ATTR = 11
F32, BF16, I32 = jnp.float32, jnp.bfloat16, jnp.int32
VMEM = 56 * 1024 * 1024


def params(*semantics):
    return pltpu.CompilerParams(vmem_limit_bytes=VMEM)


def shape(dims, dtype=F32):
    return jax.ShapeDtypeStruct(dims, dtype)


def iota(dims, dim):
    return lax.broadcasted_iota(I32, dims, dim)


def edges_kernel(v_ref, low_row, high_row, low_col, high_col):
    low_row[...] = v_ref[pl.ds(0, L, stride=Y), :]
    high_row[...] = v_ref[pl.ds(Y - 1, L, stride=Y), :]
    lane = iota((Y, X), 1)
    low = jnp.zeros((Y, X), F32)
    high = jnp.zeros((Y, X), F32)
    for l in range(L):
        turned = pltpu.roll(v_ref[pl.ds(l * Y, Y), :], l, 1)
        low = jnp.where(lane == l, turned, low)
        high = jnp.where(lane == (l + X - 1) % X, turned, high)
    low_col[...] = low
    high_col[...] = pltpu.roll(high, 1, 1)


def edges(state):
    return pl.pallas_call(
        edges_kernel,
        grid=(T,),
        in_specs=[pl.BlockSpec((L * Y, X), lambda t: (t, 0))],
        out_specs=[
            pl.BlockSpec((None, L, X), lambda t: (t, 0, 0)),
            pl.BlockSpec((None, L, X), lambda t: (t, 0, 0)),
            pl.BlockSpec((None, Y, X), lambda t: (t, 0, 0)),
            pl.BlockSpec((None, Y, X), lambda t: (t, 0, 0)),
        ],
        out_shape=[shape((T, L, X)), shape((T, L, X)), shape((T, Y, X)), shape((T, Y, X))],
        compiler_params=params(),
        name="edges",
    )(state.reshape(T * L * Y, X))


def exchange(low_row, high_row, low_col, high_col):
    lats, lons = lax.axis_size("lat"), lax.axis_size("lon")
    up = [(i, i + 1) for i in range(lats - 1)]
    down = [(b, a) for a, b in up]
    east = [(i, (i + 1) % lons) for i in range(lons)]
    west = [(b, a) for a, b in east]
    north = lax.ppermute(low_row, "lat", down)
    south = lax.ppermute(high_row, "lat", up)
    to_east = lax.ppermute(low_col, "lon", west)
    to_west = lax.ppermute(high_col, "lon", east)
    return north, south, to_east, to_west


def spread_kernel(r_ref, hi_ref, lo_ref):
    same = iota((K, K), 0) % 8 == iota((K, K), 1) % 8
    pick = jnp.where(iota((BL, K), 0) == iota((BL, K), 1) // 8, 1.0, 0.0).astype(BF16)
    for n in range(NB * YT):
        r = jnp.concatenate([r_ref[n, pl.ds(j, 8, stride=BL), :] for j in range(BL)], axis=0)
        for part, ref in zip(split(r), (hi_ref, lo_ref)):
            wide = jnp.dot(part, pick, preferred_element_type=F32)
            ref[n] = jnp.where(same, wide, 0.0).astype(BF16)


def spread(r):
    return pl.pallas_call(
        spread_kernel,
        out_shape=[shape((NB * YT, K, K), BF16)] * 2,
        compiler_params=params(),
        name="spread",
    )(r)


def transported(v, flows, north, south, to_east, to_west):
    row, lane = iota((Y, X), 0), iota((Y, X), 1)
    e = jnp.where(lane == X - 1, to_east, pltpu.roll(v, X - 1, 1))
    w = jnp.where(lane == 0, to_west, pltpu.roll(v, 1, 1))
    n = jnp.where(row == Y - 1, north, pltpu.roll(v, Y - 1, 0))
    s = jnp.where(row == 0, south, pltpu.roll(v, 1, 0))
    return v + flows[0] * (e - v) + flows[1] * (w - v) + flows[2] * (n - v) + flows[3] * (s - v)


def split(x):
    hi = x.astype(BF16)
    return hi, (x - hi.astype(F32)).astype(BF16)


def mixed(hi, lo, x):
    x_hi, x_lo = split(x)
    dot = lambda a, b: jnp.dot(a, b, preferred_element_type=F32)
    return dot(hi, x_hi) + (dot(hi, x_lo) + dot(lo, x_hi))


def step_specs():
    return [
        pl.BlockSpec((T, BL, Y, X), lambda b: (0, b, 0, 0)),
        pl.BlockSpec((4, BL, Y, X), lambda b: (0, b, 0, 0)),
        pl.BlockSpec((T, BL, X), lambda b: (0, b, 0)),
        pl.BlockSpec((T, BL, X), lambda b: (0, b, 0)),
        pl.BlockSpec((T, Y, X), lambda b: (0, 0, 0)),
        pl.BlockSpec((T, Y, X), lambda b: (0, 0, 0)),
        pl.BlockSpec((YT, K, K), lambda b: (b, 0, 0)),
        pl.BlockSpec((YT, K, K), lambda b: (b, 0, 0)),
    ]


def step_kernel(extras, v_ref, f_ref, n_ref, s_ref, e_ref, w_ref, hi_ref, lo_ref, out_ref, *rest):
    b = pl.program_id(0)
    adv = rest[-1]
    for t in range(T):
        for i in range(BL):
            l = b * BL + i
            a = transported(
                v_ref[t, i],
                [f_ref[k, i] for k in range(4)],
                n_ref[t, pl.ds(i, 1), :],
                s_ref[t, pl.ds(i, 1), :],
                pltpu.roll(e_ref[t], X - 1 - l, 1),
                pltpu.roll(w_ref[t], X - l, 1),
            )
            for q in range(YT):
                adv[q, pl.ds(i * 8, 8), pl.ds(t * X, X)] = a[q * 8 : q * 8 + 8]
    if extras:
        table, low_row, high_row, low_col, high_col, summed, _ = rest
        lane = iota((8, X), 1)

        @pl.when(b == 0)
        def _():
            low_col[...] = jnp.zeros((T, Y, X), F32)
            high_col[...] = jnp.zeros((T, Y, X), F32)

    for q in range(YT):
        out = mixed(hi_ref[q], lo_ref[q], adv[q])
        parts = [
            [out[j * 8 : j * 8 + 8, t * X : (t + 1) * X] for j in range(BL)] for t in range(T)
        ]
        for t in range(T):
            for j in range(BL):
                out_ref[t, j, pl.ds(q * 8, 8), :] = parts[t][j]
        if extras:
            here = pl.ds(q * 8, 8)
            for j in range(BL):
                summed[pl.ds(j * Y + q * 8, 8), :] = parts[0][j] + parts[1][j] + parts[2][j]
            for t in range(T):
                low, high = low_col[t, here, :], high_col[t, here, :]
                for j in range(BL):
                    l = b * BL + j
                    low = jnp.where(lane == l, pltpu.roll(parts[t][j], l, 1), low)
                    high = jnp.where(lane == l, pltpu.roll(parts[t][j], l + 1, 1), high)
                low_col[t, here, :] = low
                high_col[t, here, :] = high
    if extras:
        for y in range(Y):
            table[y] = summed[pl.ds(y, BL, stride=Y), :]
        for t in range(T):
            low_row[t] = out_ref[t, :, 0, :]
            high_row[t] = out_ref[t, :, Y - 1, :]


def full_step(state, outflow, halo, matrices, extras):
    def kernel(*refs):
        step_kernel(extras, *refs)

    out_specs = [pl.BlockSpec((T, BL, Y, X), lambda b: (0, b, 0, 0))]
    out_shape = [shape((T, L, Y, X))]
    scratch = [pltpu.VMEM((YT, K, T * X), F32)]
    if extras:
        out_specs += [
            pl.BlockSpec((Y, BL, X), lambda b: (0, b, 0)),
            pl.BlockSpec((T, BL, X), lambda b: (0, b, 0)),
            pl.BlockSpec((T, BL, X), lambda b: (0, b, 0)),
            pl.BlockSpec((T, Y, X), lambda b: (0, 0, 0)),
            pl.BlockSpec((T, Y, X), lambda b: (0, 0, 0)),
        ]
        out_shape += [
            shape((Y, L, X)),
            shape((T, L, X)),
            shape((T, L, X)),
            shape((T, Y, X)),
            shape((T, Y, X)),
        ]
        scratch = [pltpu.VMEM((BL * Y, X), F32)] + scratch
    return pl.pallas_call(
        kernel,
        grid=(NB,),
        in_specs=step_specs(),
        out_specs=out_specs,
        out_shape=out_shape,
        scratch_shapes=scratch,
        compiler_params=params(),
        name="step",
    )(state, outflow, *halo, *matrices)


def order_kernel(own_ref, col_ref, lev_ref, pc_ref, pv_ref, start_ref, count_ref, place):
    width = 256
    chunks = SND // width
    owner = iota((OWN, width), 0)
    named = lambda c: owner == own_ref[:, pl.ds(c * width, width)]
    bit = lambda m: jnp.where(m, 1.0, 0.0).astype(BF16)
    upto = bit(iota((width, width), 0) <= iota((width, width), 1))
    ones = jnp.ones((width, width), BF16)
    ones_rows = jnp.ones((16, width), BF16)
    total = jnp.zeros((OWN, width), F32)
    total_row = jnp.zeros((16, OWN), F32)
    over_lanes = (((1,), (1,)), ((), ()))
    for c in range(chunks):
        hot = bit(named(c))
        total = total + jnp.dot(hot, ones, preferred_element_type=F32)
        total_row = total_row + lax.dot_general(
            ones_rows, hot, over_lanes, preferred_element_type=F32
        )
    below = bit(iota((OWN, OWN), 1) < iota((OWN, OWN), 0))
    before = bit(iota((OWN, OWN), 0) < iota((OWN, OWN), 1))
    base = jnp.dot(below, total.astype(BF16), preferred_element_type=F32)
    start_row = jnp.dot(total_row.astype(BF16), before, preferred_element_type=F32)
    start_ref[...] = start_row[0:1].astype(I32)
    count_ref[...] = total_row[0:1].astype(I32)
    for c in range(chunks):
        m = named(c)
        hot = bit(m)
        upto_here = jnp.dot(hot, upto, preferred_element_type=F32) + base
        spot = jnp.sum(jnp.where(m, upto_here, 0.0), axis=0, keepdims=True) - 1.0
        place[:, pl.ds(c * width, width)] = spot.astype(I32)
        base = base + jnp.dot(hot, ones, preferred_element_type=F32)
    width = 512
    sorted_ = jnp.zeros((ATTR * GROUPS, 128), F32)
    for c in range(SND // width):
        here = pl.ds(c * width, width)
        spot = place[:, here]
        group = iota((GROUPS, width), 0) == spot // 128
        lane = bit(iota((128, width), 0) == spot % 128)
        rows = []
        for a in range(4):
            rows.append(col_ref[a : a + 1, here] // 128)
        for a in range(4):
            rows.append(col_ref[a : a + 1, here] % 128)
        for a in range(3):
            rows.append(lev_ref[a : a + 1, here])
        spread_rows = jnp.concatenate(
            [jnp.where(group, r.astype(F32), 0.0) for r in rows], axis=0
        ).astype(BF16)
        sorted_ = sorted_ + lax.dot_general(
            spread_rows, lane, over_lanes, preferred_element_type=F32
        )
    for a in range(4):
        y = sorted_[a * GROUPS : (a + 1) * GROUPS]
        x = sorted_[(a + 4) * GROUPS : (a + 5) * GROUPS]
        pc_ref[a] = (y * 128.0 + x).astype(I32)
        pc_ref[a + 4] = pltpu.roll(pc_ref[a], 64, 1)
    for a in range(3):
        pv_ref[a] = sorted_[(a + 8) * GROUPS : (a + 9) * GROUPS].astype(I32)
        pv_ref[a + 3] = pltpu.roll(pv_ref[a], 64, 1)


def order(owner, path_column, path_level):
    return pl.pallas_call(
        order_kernel,
        out_shape=[
            shape((8, GROUPS, 128), I32),
            shape((6, GROUPS, 128), I32),
            shape((1, OWN), I32),
            shape((1, OWN), I32),
        ],
        scratch_shapes=[pltpu.VMEM((1, SND), I32)],
        compiler_params=params(),
        name="order",
    )(owner.reshape(1, SND), path_column.T, path_level.T)


def sample_kernel(table, pc_ref, pv_ref, found):
    def sample(g, carry):
        for k in range(L // 8):
            swap = 0 if k < 5 else 1
            cols = [pc_ref[a + 4 * swap, pl.ds(g, 1), :] for a in range(4)]
            levs = [pv_ref[a + 3 * swap, pl.ds(g, 1), :] for a in range(3)]
            level = iota((8, 128), 0) + k * 8
            passed = [jnp.where(v <= level, 1, 0) for v in levs]
            element = passed[0] + passed[1] + passed[2]
            at = jnp.where(
                element < 2,
                jnp.where(element < 1, cols[0], cols[1]),
                jnp.where(element < 3, cols[2], cols[3]),
            )
            x, y = at & 127, at >> 7
            acc = jnp.zeros((8, 128), F32)
            for row in range(Y):
                got = jnp.take_along_axis(
                    table[row, k * 8 : k * 8 + 8, :], x, axis=1, mode="promise_in_bounds"
                )
                acc = jnp.where(y == row, got, acc)
            found[g, k * 8 : k * 8 + 8, :] = acc
        return carry

    lax.fori_loop(0, GROUPS, sample, 0)
    found[GROUPS] = jnp.zeros((L, 128), F32)


def sampled(table, pc, pv):
    return pl.pallas_call(
        sample_kernel,
        out_shape=shape((GROUPS + 1, L, 128)),
        compiler_params=params(),
        name="sample",
    )(table, pc, pv)


def pack_kernel(k_ref, out_ref):
    first = iota((8, 128), 1) < 64
    for pair in range(16):
        lanes = slice(pair * 128, (pair + 1) * 128)
        for k in range(5):
            low = k_ref[k * 8 : k * 8 + 8, lanes]
            if k < 4:
                high = pltpu.roll(k_ref[(k + 5) * 8 : (k + 6) * 8, lanes], 64, 1)
            else:
                high = jnp.zeros((8, 128), F32)
            out_ref[2 * pair, k * 8 : k * 8 + 8, :] = jnp.where(first, low, high)
            out_ref[2 * pair + 1, k * 8 : k * 8 + 8, :] = jnp.where(first, high, low)


def packed_weights(weights):
    return pl.pallas_call(
        pack_kernel,
        grid=(OWN // 32,),
        in_specs=[pl.BlockSpec((L, 2048), lambda i: (0, i))],
        out_specs=pl.BlockSpec((32, ROWS, 128), lambda i: (i, 0, 0)),
        out_shape=shape((OWN, ROWS, 128)),
        compiler_params=params(),
        name="pack",
    )(weights)


def weigh_kernel(start_ref, count_ref, half_ref, found, k_ref, out_ref, kept):
    lane = iota((8, 128), 1)
    step = pl.program_id(0)
    for n in range(16):
        o = step * 16 + n
        start, count = start_ref[0, o], count_ref[0, o]
        group, offset = jnp.minimum(start // 128, GROUPS - 1), start % 128
        near = lane >= offset
        near_high = (lane ^ 64) >= offset
        low = ((lane - offset) & 127) < 64
        acc = jnp.zeros((8, 128), F32)
        for k in range(5):
            rows = slice(k * 8, k * 8 + 8)
            z = jnp.where(near, found[group, rows, :], found[group + 1, rows, :])
            if k < 4:
                rows_high = slice((k + 5) * 8, (k + 6) * 8)
                z_high = jnp.where(
                    near_high, found[group, rows_high, :], found[group + 1, rows_high, :]
                )
                z = jnp.where(low, z, z_high)
            turned = pltpu.roll(z, (half_ref[0] + 128 - offset) % 128, 1)
            acc = acc + turned * k_ref[n, rows, :]
        kept[pl.ds(n * 8, 8), :] = jnp.where((lane & 63) < count, acc, 0.0)
    total = kept[pl.ds(0, 16, stride=8), :]
    for r in range(1, 8):
        total = total + kept[pl.ds(r, 16, stride=8), :]
    out_ref[...] = total + pltpu.roll(total, 64, 1)


def weigh(start, count, half, found, arrived):
    smem = pl.BlockSpec(memory_space=pltpu.SMEM)
    return pl.pallas_call(
        weigh_kernel,
        grid=(OWN // 16,),
        in_specs=[
            smem,
            smem,
            smem,
            pl.BlockSpec((GROUPS + 1, L, 128), lambda i: (0, 0, 0)),
            pl.BlockSpec((16, ROWS, 128), lambda i: (i, 0, 0)),
        ],
        out_specs=pl.BlockSpec((16, 128), lambda i: (i, 0)),
        out_shape=shape((OWN, 128)),
        scratch_shapes=[pltpu.VMEM((128, 128), F32)],
        compiler_params=params(),
        name="weigh",
    )(start, count, half, found, arrived)


def body(state, outflow, mix_blocks, owner, path_column, path_level, weights):
    axes = ("lon", "lat")
    sides = edges(state)
    halo = exchange(*sides)
    packed, halo = lax.optimization_barrier((packed_weights(weights), halo))
    arrived = lax.all_to_all(packed, axes, 0, 0, tiled=True)
    rows = mix_blocks.reshape(YT, 8, NB, BL, BL).transpose(2, 0, 1, 4, 3)
    matrices = spread(rows.reshape(NB * YT, K, BL))
    pc, pv, start, count = order(owner, path_column, path_level)
    half = (lax.axis_index("lat") % 2 * 64).astype(I32).reshape(1)
    first, table, *sides = full_step(state, outflow, halo, matrices, True)
    found = sampled(table, pc, pv)
    sums = weigh(start, count, half, found, arrived)
    sensitivity = lax.all_to_all(sums, axes, 0, 0, tiled=True)[:, :CAP]
    (final,) = full_step(first, outflow, exchange(*sides), matrices, False)
    return final, sensitivity.reshape(OWN * CAP)


def solution(mesh):
    return jax.shard_map(
        body,
        mesh=mesh,
        in_specs=(
            P(None, None, "lat", "lon"),
            P(None, None, "lat", "lon"),
            P("lat", None, None, None),
            P(("lon", "lat"), None),
            P(("lon", "lat"), None),
            P(("lon", "lat"), None),
            P(None, ("lon", "lat")),
        ),
        out_specs=(P(None, None, "lat", "lon"), P(("lon", "lat"))),
        check_vma=False,
    )
```

profile of v0, /device:TPU:0, one launch (start us, length us, event | category | flops | bytes accessed | tf_op | source)
XLA Modules:
  0.0 113.6 jit_solution(8429606205403534690)
XLA Ops:
  0.6 4.0 %edges.1 = (f32[3,72,128]{2,1,0:T(8,128)}, f32[3,72,128]{2,1,0:T(8,128)}, f32[3,32,128]{2,1,0:T(8,128)}, f32[3,32,128]{2,1,0:T(8,128)}) custom-call(f32[6912,128]{1,0:T(8,128)} %bitcast.15), custom_call_target="tpu_custom_call" | custom-call | tf_op jit(solution)/shard_map/edges/pallas_call | solution.py:46
  4.7 1.3 %collective-permute-start = (f32[3,72,128]{2,1,0:T(8,128)}, f32[3,72,128]{2,1,0:T(8,128)}, u32[]{:S(2)}, u32[]{:S(2)}) collective-permute-start(f32[3,72,128]{2,1,0:T(8,128)} %get-tuple-element.23), channel_id=1, source_target_pairs={{1,0},{2,1},{3,2},{4,3},{5,4},{6,5},{7,6},{9,8},{10,9},{11,10},{12... | collective-permute-start | bytes 331784 | tf_op jit(solution)/shard_map/ppermute | solution.py:68
  6.0 5.2 %collective-permute-start.1 = (f32[3,72,128]{2,1,0:T(8,128)}, f32[3,72,128]{2,1,0:T(8,128)}, u32[]{:S(2)}, u32[]{:S(2)}) collective-permute-start(f32[3,72,128]{2,1,0:T(8,128)} %get-tuple-element.24), channel_id=1, source_target_pairs={{0,1},{1,2},{2,3},{3,4},{4,5},{5,6},{6,7},{8,9},{9,10},{10,11},{11... | collective-permute-start | bytes 331784 | tf_op jit(solution)/shard_map/ppermute | solution.py:69
  11.1 5.3 %collective-permute-start.2 = (f32[3,32,128]{2,1,0:T(8,128)}, f32[3,32,128]{2,1,0:T(8,128)S(1)}, u32[]{:S(2)}, u32[]{:S(2)}) collective-permute-start(f32[3,32,128]{2,1,0:T(8,128)} %get-tuple-element.25), channel_id=1, source_target_pairs={{8,0},{16,8},{24,16},{32,24},{40,32},{48,40},{56,48},{64,56},{72,6... | collective-permute-start | bytes 147464 | tf_op jit(solution)/shard_map/ppermute | solution.py:70
  16.4 0.0 collective-permute-start.3
  16.4 4.1 %pack.1 = f32[128,40,128]{2,1,0:T(8,128)} custom-call(f32[72,8192]{1,0:T(8,128)} %k_ref.1), custom_call_target="tpu_custom_call" | custom-call | tf_op jit(solution)/shard_map/pack/pallas_call | solution.py:343
  20.6 0.0 copy-start.1
  20.6 0.0 collective-permute-done.2.refs_4_
  20.6 0.0 copy-start.4
  20.6 3.3 %collective-permute-done.3.refs_5_ = f32[3,32,128]{2,1,0:T(8,128)} collective-permute-done((f32[3,32,128]{2,1,0:T(8,128)}, f32[3,32,128]{2,1,0:T(8,128)}, u32[]{:S(2)}, u32[]{:S(2)}) %collective-permute-start.3) | collective-permute-done | bytes 49184 | tf_op jit(solution)/shard_map/ppermute | solution.py:71
  23.9 0.0 collective-permute-done.refs_2_
  23.9 0.0 collective-permute-done.1.refs_3_
  23.9 7.0 %all-to-all-start = ((f32[128,40,128]{2,1,0:T(8,128)}), f32[128,40,128]{2,1,0:T(8,128)S(1)}, u32[]{:S(2)}, u32[]{:S(2)}) async-start(f32[128,40,128]{2,1,0:T(8,128)} %pack.1), calls=%async_computation | async-start | bytes 5242880 | tf_op jit(solution)/shard_map/all_to_all | solution.py:408
  30.9 0.0 copy-done.1
  30.9 1.4 %copy.15 = f32[32,3,24,24]{2,3,0,1:T(8,128)} copy(f32[32,3,24,24]{0,3,2,1:T(8,128)S(1)} %copy-done.1) | data formatting | bytes 442368 | tf_op jit(solution)/shard_map/transpose | solution.py:409
  32.3 0.0 copy-done.4
  32.3 3.5 %spread.1 = (bf16[12,192,192]{2,1,0:T(8,128)(2,1)}, bf16[12,192,192]{2,1,0:T(8,128)(2,1)}) custom-call(f32[12,192,24]{2,1,0:T(8,128)} %bitcast.16), custom_call_target="tpu_custom_call" | custom-call | tf_op jit(solution)/shard_map/spread/pallas_call | solution.py:86
  35.8 10.7 %step.2 = (f32[3,72,32,128]{3,2,1,0:T(8,128)}, f32[32,72,128]{2,1,0:T(8,128)}, f32[3,72,128]{2,1,0:T(8,128)}, f32[3,72,128]{2,1,0:T(8,128)}, f32[3,32,128]{2,1,0:T(8,128)}, /*index=5*/f32[3,32,128]{2,1,0:T(8,128)}) custom-call(f32[3,72,32,128]{3,2,1,0:T(8,128)} %refs_0_.1, f32[4,72,32,128]{3,2,1,0:T(8,128)} %refs_1_.3, ...), custom_call_target="tpu_custom_call" | custom-call | tf_op jit(solution)/shard_map/step/pallas_call | solution.py:203
  46.5 1.3 %collective-permute-start.4 = (f32[3,72,128]{2,1,0:T(8,128)}, f32[3,72,128]{2,1,0:T(8,128)S(1)}, u32[]{:S(2)}, u32[]{:S(2)}) collective-permute-start(f32[3,72,128]{2,1,0:T(8,128)} %get-tuple-element.34), channel_id=1, source_target_pairs={{1,0},{2,1},{3,2},{4,3},{5,4},{6,5},{7,6},{9,8},{10,9},{11,10},{12... | collective-permute-start | bytes 331784 | tf_op jit(solution)/shard_map/ppermute | solution.py:68
  47.8 4.6 %collective-permute-start.5 = (f32[3,72,128]{2,1,0:T(8,128)}, f32[3,72,128]{2,1,0:T(8,128)S(1)}, u32[]{:S(2)}, u32[]{:S(2)}) collective-permute-start(f32[3,72,128]{2,1,0:T(8,128)} %get-tuple-element.35), channel_id=1, source_target_pairs={{0,1},{1,2},{2,3},{3,4},{4,5},{5,6},{6,7},{8,9},{9,10},{10,11},{11... | collective-permute-start | bytes 331784 | tf_op jit(solution)/shard_map/ppermute | solution.py:69
  52.4 4.1 %order.1 = (s32[8,32,128]{2,1,0:T(8,128)}, s32[6,32,128]{2,1,0:T(8,128)}, s32[1,128]{1,0:T(1,128)}, s32[1,128]{1,0:T(1,128)}) custom-call(s32[1,4096]{1,0:T(1,128)} %bitcast.21, s32[4,4096]{1,0:T(4,128)} %bitcast.19, s32[3,4096]{1,0:T(4,128)} %bitcast.20), custom_call_target="tpu_custom_call" | custom-call | tf_op jit(solution)/shard_map/order/pallas_call | solution.py:277
  56.5 15.5 %sample.1.found = f32[33,72,128]{2,1,0:T(8,128)} custom-call(f32[32,72,128]{2,1,0:T(8,128)} %get-tuple-element.40.table, s32[8,32,128]{2,1,0:T(8,128)} %get-tuple-element.41.pc_ref, s32[6,32,128]{2,1,0:T(8,128)} %get-tuple-element.42.pv_ref), custom_call_target="tpu_custom_call" | custom-call | tf_op jit(solution)/shard_map/sample/pallas_call | solution.py:320
  71.9 0.0 copy-start.8
  71.9 0.0 copy-start.7
  71.9 0.0 all-to-all-done.k_ref
  71.9 0.0 copy-start
  71.9 1.5 %copy-done = f32[128,40,128]{2,1,0:T(8,128)} copy-done((f32[128,40,128]{2,1,0:T(8,128)}, f32[128,40,128]{2,1,0:T(8,128)S(1)}, u32[]{:S(2)}) %copy-start) | copy-done | bytes 2621464
  73.4 7.1 %weigh.1 = f32[128,128]{1,0:T(8,128)} custom-call(s32[1,128]{1,0:T(1,128)} %get-tuple-element.38.start_ref, s32[1,128]{1,0:T(1,128)} %get-tuple-element.39.count_ref, s32[1]{0:T(128)} %bitcast.8.half_ref, f32[33,72,128]{2,1,0:T(8,128)} %sample.1.found, f32[128,40,128]{2,1,0:T(8,128)} %copy-done), custom_call_target="tpu_custom_call" | custom-call | tf_op jit(solution)/shard_map/weigh/pallas_call | solution.py:385
  80.6 10.6 %all-to-all-start.1 = ((f32[128,1,128]{2,1,0:T(1,128)}), f32[128,1,128]{2,1,0:T(1,128)S(1)}, u32[]{:S(2)}, u32[]{:S(2)}) async-start(f32[128,1,128]{2,1,0:T(1,128)} %bitcast.17), calls=%async_computation.1 | async-start | bytes 131072 | tf_op jit(solution)/shard_map/all_to_all | solution.py:416
  91.2 0.0 copy-done.8
  91.2 5.0 %collective-permute-start.6 = (f32[3,32,128]{2,1,0:T(8,128)S(1)}, f32[3,32,128]{2,1,0:T(8,128)S(1)}, u32[]{:S(2)}, u32[]{:S(2)}) collective-permute-start(f32[3,32,128]{2,1,0:T(8,128)S(1)} %copy-done.8), channel_id=1, source_target_pairs={{8,0},{16,8},{24,16},{32,24},{40,32},{48,40},{56,48},{64,56},{72,6... | collective-permute-start | bytes 147464 | tf_op jit(solution)/shard_map/ppermute | solution.py:70
  96.2 0.0 copy-done.7
  96.2 0.0 collective-permute-start.7
  96.2 1.7 %collective-permute-done.6.refs_4_ = f32[3,32,128]{2,1,0:T(8,128)S(1)} collective-permute-done((f32[3,32,128]{2,1,0:T(8,128)S(1)}, f32[3,32,128]{2,1,0:T(8,128)S(1)}, u32[]{:S(2)}, u32[]{:S(2)}) %collective-permute-start.6) | collective-permute-done | bytes 49184 | tf_op jit(solution)/shard_map/ppermute | solution.py:70
  98.0 0.0 copy-start.5
  98.0 5.4 %collective-permute-done.7.refs_5_ = f32[3,32,128]{2,1,0:T(8,128)S(1)} collective-permute-done((f32[3,32,128]{2,1,0:T(8,128)S(1)}, f32[3,32,128]{2,1,0:T(8,128)S(1)}, u32[]{:S(2)}, u32[]{:S(2)}) %collective-permute-start.7) | collective-permute-done | bytes 49184 | tf_op jit(solution)/shard_map/ppermute | solution.py:71
  103.4 0.0 copy-start.6
  103.4 0.0 collective-permute-done.4.refs_2_
  103.4 0.0 copy-start.2
  103.4 0.0 collective-permute-done.5.refs_3_
  103.4 0.0 copy-start.3
  103.4 0.0 copy-done.5
  103.4 0.6 copy-done.6
  104.0 0.0 copy-done.2
  104.0 0.1 copy-done.3
  104.1 8.8 %step.3 = f32[3,72,32,128]{3,2,1,0:T(8,128)} custom-call(f32[3,72,32,128]{3,2,1,0:T(8,128)} %get-tuple-element.33.refs_0_, f32[4,72,32,128]{3,2,1,0:T(8,128)} %refs_1_.3, f32[3,72,128]{2,1,0:T(8,128)} %copy-done.2, f32[3,72,128]{2,1,0:T(8,128)} %copy-done.3, f32[3,32,128]{2,1,0:T(8,128)} %copy-done.5, f32[3,32,128]{2,1,0:T(8,128)} %copy-done.6, ...), custom_call_target="tpu_custom_call" | custom-call | tf_op jit(solution)/shard_map/step/pallas_call | solution.py:203
  112.9 0.0 all-to-all-done.1
  112.9 0.7 reshape.29
Async XLA Ops:
  4.7 19.2 %collective-permute-start = (f32[3,72,128]{2,1,0:T(8,128)}, f32[3,72,128]{2,1,0:T(8,128)}, u32[]{:S(2)}, u32[]{:S(2)}) collective-permute-start(f32[3,72,128]{2,1,0:T(8,128)} %get-tuple-element.23), channel_id=1, source_target_pairs={{1,0},{2,1},{3,2},{4,3},{5,4},{6,5},{7,6},{9,8},{10,9},{11,10},{12... | collective-permute-start | bytes 331784 | tf_op jit(solution)/shard_map/ppermute | solution.py:68
  6.0 17.9 %collective-permute-start.1 = (f32[3,72,128]{2,1,0:T(8,128)}, f32[3,72,128]{2,1,0:T(8,128)}, u32[]{:S(2)}, u32[]{:S(2)}) collective-permute-start(f32[3,72,128]{2,1,0:T(8,128)} %get-tuple-element.24), channel_id=1, source_target_pairs={{0,1},{1,2},{2,3},{3,4},{4,5},{5,6},{6,7},{8,9},{9,10},{10,11},{11... | collective-permute-start | bytes 331784 | tf_op jit(solution)/shard_map/ppermute | solution.py:69
  11.1 9.4 %collective-permute-start.2 = (f32[3,32,128]{2,1,0:T(8,128)}, f32[3,32,128]{2,1,0:T(8,128)S(1)}, u32[]{:S(2)}, u32[]{:S(2)}) collective-permute-start(f32[3,32,128]{2,1,0:T(8,128)} %get-tuple-element.25), channel_id=1, source_target_pairs={{8,0},{16,8},{24,16},{32,24},{40,32},{48,40},{56,48},{64,56},{72,6... | collective-permute-start | bytes 147464 | tf_op jit(solution)/shard_map/ppermute | solution.py:70
  16.4 7.4 %collective-permute-start.3 = (f32[3,32,128]{2,1,0:T(8,128)}, f32[3,32,128]{2,1,0:T(8,128)}, u32[]{:S(2)}, u32[]{:S(2)}) collective-permute-start(f32[3,32,128]{2,1,0:T(8,128)} %get-tuple-element.26), channel_id=1, source_target_pairs={{0,8},{8,16},{16,24},{24,32},{32,40},{40,48},{48,56},{56,64},{64,7... | collective-permute-start | bytes 147464 | tf_op jit(solution)/shard_map/ppermute | solution.py:71
  20.6 10.3 %copy-start.1 = (f32[32,3,24,24]{0,3,2,1:T(8,128)S(1)}, f32[32,3,24,24]{0,3,2,1:T(8,128)}, u32[]{:S(2)}) copy-start(f32[32,3,24,24]{0,3,2,1:T(8,128)} %param.9) | copy-start | bytes 663556
  20.6 11.8 %copy-start.4 = (f32[3,32,128]{2,1,0:T(8,128)}, f32[3,32,128]{2,1,0:T(8,128)S(1)}, u32[]{:S(2)}) copy-start(f32[3,32,128]{2,1,0:T(8,128)S(1)} %collective-permute-done.2.refs_4_) | copy-start | bytes 147460
  23.9 48.0 %all-to-all-start = ((f32[128,40,128]{2,1,0:T(8,128)}), f32[128,40,128]{2,1,0:T(8,128)S(1)}, u32[]{:S(2)}, u32[]{:S(2)}) async-start(f32[128,40,128]{2,1,0:T(8,128)} %pack.1), calls=%async_computation | async-start | bytes 5242880 | tf_op jit(solution)/shard_map/all_to_all | solution.py:408
  46.5 56.8 %collective-permute-start.4 = (f32[3,72,128]{2,1,0:T(8,128)}, f32[3,72,128]{2,1,0:T(8,128)S(1)}, u32[]{:S(2)}, u32[]{:S(2)}) collective-permute-start(f32[3,72,128]{2,1,0:T(8,128)} %get-tuple-element.34), channel_id=1, source_target_pairs={{1,0},{2,1},{3,2},{4,3},{5,4},{6,5},{7,6},{9,8},{10,9},{11,10},{12... | collective-permute-start | bytes 331784 | tf_op jit(solution)/shard_map/ppermute | solution.py:68
  47.8 55.6 %collective-permute-start.5 = (f32[3,72,128]{2,1,0:T(8,128)}, f32[3,72,128]{2,1,0:T(8,128)S(1)}, u32[]{:S(2)}, u32[]{:S(2)}) collective-permute-start(f32[3,72,128]{2,1,0:T(8,128)} %get-tuple-element.35), channel_id=1, source_target_pairs={{0,1},{1,2},{2,3},{3,4},{4,5},{5,6},{6,7},{8,9},{9,10},{10,11},{11... | collective-permute-start | bytes 331784 | tf_op jit(solution)/shard_map/ppermute | solution.py:69
  71.9 19.3 %copy-start.8 = (f32[3,32,128]{2,1,0:T(8,128)S(1)}, f32[3,32,128]{2,1,0:T(8,128)}, u32[]{:S(2)}) copy-start(f32[3,32,128]{2,1,0:T(8,128)} %get-tuple-element.36) | copy-start | bytes 147460
  71.9 24.3 %copy-start.7 = (f32[3,32,128]{2,1,0:T(8,128)S(1)}, f32[3,32,128]{2,1,0:T(8,128)}, u32[]{:S(2)}) copy-start(f32[3,32,128]{2,1,0:T(8,128)} %get-tuple-element.37) | copy-start | bytes 147460
  71.9 1.5 %copy-start = (f32[128,40,128]{2,1,0:T(8,128)}, f32[128,40,128]{2,1,0:T(8,128)S(1)}, u32[]{:S(2)}) copy-start(f32[128,40,128]{2,1,0:T(8,128)S(1)} %all-to-all-done.k_ref) | copy-start | bytes 7864324
  80.6 32.3 %all-to-all-start.1 = ((f32[128,1,128]{2,1,0:T(1,128)}), f32[128,1,128]{2,1,0:T(1,128)S(1)}, u32[]{:S(2)}, u32[]{:S(2)}) async-start(f32[128,1,128]{2,1,0:T(1,128)} %bitcast.17), calls=%async_computation.1 | async-start | bytes 131072 | tf_op jit(solution)/shard_map/all_to_all | solution.py:416
  91.2 6.7 %collective-permute-start.6 = (f32[3,32,128]{2,1,0:T(8,128)S(1)}, f32[3,32,128]{2,1,0:T(8,128)S(1)}, u32[]{:S(2)}, u32[]{:S(2)}) collective-permute-start(f32[3,32,128]{2,1,0:T(8,128)S(1)} %copy-done.8), channel_id=1, source_target_pairs={{8,0},{16,8},{24,16},{32,24},{40,32},{48,40},{56,48},{64,56},{72,6... | collective-permute-start | bytes 147464 | tf_op jit(solution)/shard_map/ppermute | solution.py:70
  96.2 7.1 %collective-permute-start.7 = (f32[3,32,128]{2,1,0:T(8,128)S(1)}, f32[3,32,128]{2,1,0:T(8,128)S(1)}, u32[]{:S(2)}, u32[]{:S(2)}) collective-permute-start(f32[3,32,128]{2,1,0:T(8,128)S(1)} %copy-done.7), channel_id=1, source_target_pairs={{0,8},{8,16},{16,24},{24,32},{32,40},{40,48},{48,56},{56,64},{64,7... | collective-permute-start | bytes 147464 | tf_op jit(solution)/shard_map/ppermute | solution.py:71
  98.0 5.4 %copy-start.5 = (f32[3,32,128]{2,1,0:T(8,128)}, f32[3,32,128]{2,1,0:T(8,128)S(1)}, u32[]{:S(2)}) copy-start(f32[3,32,128]{2,1,0:T(8,128)S(1)} %collective-permute-done.6.refs_4_) | copy-start | bytes 147460
  103.4 0.6 copy-start.6
  103.4 0.7 copy-start.2
  103.4 0.7 copy-start.3
where the time goes:
time: 114 us
  Pallas kernels  57.9 us (51%)
  starting transfers between devices  40.2 us (35%)
  waiting for transfers between devices  10.5 us (9%)
  local copies, waits for them, and re-layouts  4.33 us (4%)
    pallas_call x2, Pallas kernels, full_step(): pl.pallas_call(kernel, grid=(NB,), in_specs=step_specs(), out_specs=out_s...  19.5 us
    pallas_call x1, Pallas kernels, sampled(): pl.pallas_call(sample_kernel, out_shape=shape((GROUPS + 1, L, 128)), comp...  15.5 us
    all_to_all x1, starting transfers between devices, body(): sensitivity = lax.all_to_all(sums, axes, 0, 0, tiled=True)[:, :CAP]  10.6 us
    ppermute x2, starting transfers between devices, exchange(): to_east = lax.ppermute(low_col, 'lon', west)  10.3 us
    ppermute x2, starting transfers between devices, exchange(): south = lax.ppermute(high_row, 'lat', up)  9.74 us
    ppermute x2, waiting for transfers between devices, exchange(): to_west = lax.ppermute(high_col, 'lon', east)  8.7 us
    pallas_call x1, Pallas kernels, weigh(): pl.pallas_call(weigh_kernel, grid=(OWN // 16,), in_specs=[smem, smem, sme...  7.15 us
    all_to_all x1, starting transfers between devices, body(): arrived = lax.all_to_all(packed, axes, 0, 0, tiled=True)  6.96 us
  transfers between devices with their start and end apart: 10, of which 3 were waited for; matrix products, arithmetic and copies ran while one was open for 1% of the time, Pallas kernels for 47%

commit v1 on v0

v1 whole, which is shorter than its diff:
```python
import jax
import jax.numpy as jnp
from jax import lax
from jax.experimental import pallas as pl
from jax.experimental.pallas import tpu as pltpu
from jax.sharding import PartitionSpec as P

T, L, NB, BL, Y, X = 3, 72, 3, 24, 32, 128
OWN, CAP, SND = 128, 64, 4096
YT = Y // 8
K = 8 * BL
ROWS = 40
GROUPS = SND // 128
ATTR = 11
F32, BF16, I32 = jnp.float32, jnp.bfloat16, jnp.int32
VMEM = 63 * 1024 * 1024


def params(*semantics):
    return pltpu.CompilerParams(vmem_limit_bytes=VMEM)


def shape(dims, dtype=F32):
    return jax.ShapeDtypeStruct(dims, dtype)


def iota(dims, dim):
    return lax.broadcasted_iota(I32, dims, dim)


def copies(pairs, sems):
    return [pltpu.make_async_copy(src, dst, sems.at[n]) for n, (src, dst) in enumerate(pairs)]


ANY = pl.BlockSpec(memory_space=pl.ANY)
IN_VMEM = pl.BlockSpec(memory_space=pltpu.VMEM)
IN_SMEM = pl.BlockSpec(memory_space=pltpu.SMEM)


def edge_columns(parts):
    lane = iota((parts[0].shape[0], X), 1)
    both = jnp.zeros(lane.shape, F32)
    for i, part in enumerate(parts):
        both = jnp.where(lane >> 1 == i, pltpu.roll(part, 2 * i + 1, 1), both)
    return both


PACKS = 4


def prepare_kernel(v_hbm, k_hbm, low_row, high_row, cols, packed_hbm, v, k, packed, v_sem, k_sem, p_sem):
    wide = OWN * CAP // PACKS
    deep = OWN // PACKS
    v_in = copies([(v_hbm.at[t], v.at[t]) for t in range(T)], v_sem)
    k_in = copies([(k_hbm.at[:, pl.ds(n * wide, wide)], k.at[n]) for n in range(PACKS)], k_sem)
    out = copies(
        [(packed.at[n], packed_hbm.at[pl.ds(n * deep, deep)]) for n in range(PACKS)], p_sem
    )
    for c in v_in + k_in:
        c.start()
    for t in range(T):
        v_in[t].wait()
        low_row[t] = v[t, pl.ds(0, L, stride=Y), :]
        high_row[t] = v[t, pl.ds(Y - 1, L, stride=Y), :]
        for b in range(NB):
            cols[b, t] = edge_columns([v[t, pl.ds((b * BL + i) * Y, Y), :] for i in range(BL)])
    first = iota((8, 128), 1) < 64
    for n in range(PACKS):
        k_in[n].wait()
        for pair in range(deep // 2):
            lanes = slice(pair * 128, (pair + 1) * 128)
            for r in range(5):
                low = k[n, r * 8 : r * 8 + 8, lanes]
                if r < 4:
                    high = pltpu.roll(k[n, (r + 5) * 8 : (r + 6) * 8, lanes], 64, 1)
                else:
                    high = jnp.zeros((8, 128), F32)
                packed[n, 2 * pair, r * 8 : r * 8 + 8, :] = jnp.where(first, low, high)
                packed[n, 2 * pair + 1, r * 8 : r * 8 + 8, :] = jnp.where(first, high, low)
        out[n].start()
    for c in out:
        c.wait()


def prepare(state, weights):
    return pl.pallas_call(
        prepare_kernel,
        in_specs=[ANY, ANY],
        out_specs=[IN_VMEM, IN_VMEM, IN_VMEM, ANY],
        out_shape=[
            shape((T, L, X)),
            shape((T, L, X)),
            shape((NB, T, Y, X)),
            shape((OWN, ROWS, 128)),
        ],
        scratch_shapes=[
            pltpu.VMEM((T, L * Y, X), F32),
            pltpu.VMEM((PACKS, L, OWN * CAP // PACKS), F32),
            pltpu.VMEM((PACKS, OWN // PACKS, ROWS, 128), F32),
            pltpu.SemaphoreType.DMA((T,)),
            pltpu.SemaphoreType.DMA((PACKS,)),
            pltpu.SemaphoreType.DMA((PACKS,)),
        ],
        compiler_params=params(),
        name="prepare",
    )(state.reshape(T, L * Y, X), weights)


def exchange(low_row, high_row, cols):
    lats, lons = lax.axis_size("lat"), lax.axis_size("lon")
    up = [(i, i + 1) for i in range(lats - 1)]
    down = [(b, a) for a, b in up]
    east = [(i, (i + 1) % lons) for i in range(lons)]
    west = [(b, a) for a, b in east]
    north = lax.ppermute(low_row, "lat", down)
    south = lax.ppermute(high_row, "lat", up)
    from_east = lax.ppermute(cols, "lon", west)
    from_west = lax.ppermute(cols, "lon", east)
    return north, south, from_east, from_west


def split(x):
    hi = x.astype(BF16)
    return hi, (x - hi.astype(F32)).astype(BF16)


def spread(r_ref, hi_ref, lo_ref):
    same = iota((K, K), 0) % 8 == iota((K, K), 1) % 8
    pick = jnp.where(iota((BL, K), 0) == iota((BL, K), 1) // 8, 1.0, 0.0).astype(BF16)
    for n in range(NB * YT):
        r = jnp.concatenate([r_ref[n, pl.ds(j, 8, stride=BL), :] for j in range(BL)], axis=0)
        for part, ref in zip(split(r), (hi_ref, lo_ref)):
            wide = jnp.dot(part, pick, preferred_element_type=F32)
            ref[n] = jnp.where(same, wide, 0.0).astype(BF16)


def transported(v, flows, north, south, sides):
    row, lane = iota((Y, X), 0), iota((Y, X), 1)
    e = pltpu.roll(jnp.where(lane == 0, sides, v), X - 1, 1)
    w = pltpu.roll(jnp.where(lane == X - 1, sides, v), 1, 1)
    n = jnp.where(row == Y - 1, north, pltpu.roll(v, Y - 1, 0))
    s = jnp.where(row == 0, south, pltpu.roll(v, 1, 0))
    return v + flows[0] * (e - v) + flows[1] * (w - v) + flows[2] * (n - v) + flows[3] * (s - v)


def mixed(hi, lo, x):
    x_hi, x_lo = split(x)
    dot = lambda a, b: jnp.dot(a, b, preferred_element_type=F32)
    return dot(hi, x_hi) + (dot(hi, x_lo) + dot(lo, x_hi))


def transport_block(adv, v, f, n_ref, s_ref, e_ref, w_ref):
    odd = (iota((Y, X), 1) & 1) == 1
    for t in range(T):
        sides = jnp.where(odd, e_ref[t], w_ref[t])
        for i in range(BL):
            a = transported(
                v[t, i],
                [f[k, i] for k in range(4)],
                n_ref[t, pl.ds(i, 1), :],
                s_ref[t, pl.ds(i, 1), :],
                pltpu.roll(sides, (X - 2 * i - 1) % X, 1),
            )
            for q in range(YT):
                adv[q, pl.ds(i * 8, 8), pl.ds(t * X, X)] = a[q * 8 : q * 8 + 8]


def tiles(out):
    return [[out[j * 8 : j * 8 + 8, t * X : (t + 1) * X] for j in range(BL)] for t in range(T)]


def last_kernel(v_ref, f_ref, n_ref, s_ref, e_ref, w_ref, hi_ref, lo_ref, out_ref, adv):
    transport_block(adv, v_ref, f_ref, n_ref, s_ref, e_ref, w_ref)
    for q in range(YT):
        parts = tiles(mixed(hi_ref[q], lo_ref[q], adv[q]))
        for t in range(T):
            for j in range(BL):
                out_ref[t, j, pl.ds(q * 8, 8), :] = parts[t][j]


def last_step(state, outflow, halo, matrices):
    return pl.pallas_call(
        last_kernel,
        grid=(NB,),
        in_specs=[
            pl.BlockSpec((T, BL, Y, X), lambda b: (0, b, 0, 0)),
            pl.BlockSpec((4, BL, Y, X), lambda b: (0, b, 0, 0)),
            pl.BlockSpec((T, BL, X), lambda b: (0, b, 0)),
            pl.BlockSpec((T, BL, X), lambda b: (0, b, 0)),
            pl.BlockSpec((None, T, Y, X), lambda b: (b, 0, 0, 0)),
            pl.BlockSpec((None, T, Y, X), lambda b: (b, 0, 0, 0)),
            pl.BlockSpec((YT, K, K), lambda b: (b, 0, 0)),
            pl.BlockSpec((YT, K, K), lambda b: (b, 0, 0)),
        ],
        out_specs=pl.BlockSpec((T, BL, Y, X), lambda b: (0, b, 0, 0)),
        out_shape=shape((T, L, Y, X)),
        scratch_shapes=[pltpu.VMEM((YT, K, T * X), F32)],
        compiler_params=params(),
        name="last_step",
    )(state, outflow, *halo, *matrices)


def order(own_ref, col_ref, lev_ref, pc_ref, pv_ref, start_ref, count_ref, place):
    width = 256
    chunks = SND // width
    owner = iota((OWN, width), 0)
    named = lambda c: owner == own_ref[:, pl.ds(c * width, width)]
    bit = lambda m: jnp.where(m, 1.0, 0.0).astype(BF16)
    upto = bit(iota((width, width), 0) <= iota((width, width), 1))
    ones = jnp.ones((width, width), BF16)
    ones_rows = jnp.ones((16, width), BF16)
    total = jnp.zeros((OWN, width), F32)
    total_row = jnp.zeros((16, OWN), F32)
    over_lanes = (((1,), (1,)), ((), ()))
    for c in range(chunks):
        hot = bit(named(c))
        total = total + jnp.dot(hot, ones, preferred_element_type=F32)
        total_row = total_row + lax.dot_general(
            ones_rows, hot, over_lanes, preferred_element_type=F32
        )
    below = bit(iota((OWN, OWN), 1) < iota((OWN, OWN), 0))
    before = bit(iota((OWN, OWN), 0) < iota((OWN, OWN), 1))
    base = jnp.dot(below, total.astype(BF16), preferred_element_type=F32)
    start_row = jnp.dot(total_row.astype(BF16), before, preferred_element_type=F32)
    start_ref[...] = start_row[0:1].astype(I32)
    count_ref[...] = total_row[0:1].astype(I32)
    for c in range(chunks):
        m = named(c)
        hot = bit(m)
        upto_here = jnp.dot(hot, upto, preferred_element_type=F32) + base
        spot = jnp.sum(jnp.where(m, upto_here, 0.0), axis=0, keepdims=True) - 1.0
        place[:, pl.ds(c * width, width)] = spot.astype(I32)
        base = base + jnp.dot(hot, ones, preferred_element_type=F32)
    width = 512
    sorted_ = jnp.zeros((ATTR * GROUPS, 128), F32)
    for c in range(SND // width):
        here = pl.ds(c * width, width)
        spot = place[:, here]
        group = iota((GROUPS, width), 0) == spot // 128
        lane = bit(iota((128, width), 0) == spot % 128)
        rows = []
        for a in range(4):
            rows.append(col_ref[a : a + 1, here] // 128)
        for a in range(4):
            rows.append(col_ref[a : a + 1, here] % 128)
        for a in range(3):
            rows.append(lev_ref[a : a + 1, here])
        spread_rows = jnp.concatenate(
            [jnp.where(group, r.astype(F32), 0.0) for r in rows], axis=0
        ).astype(BF16)
        sorted_ = sorted_ + lax.dot_general(
            spread_rows, lane, over_lanes, preferred_element_type=F32
        )
    for a in range(4):
        y = sorted_[a * GROUPS : (a + 1) * GROUPS]
        x = sorted_[(a + 4) * GROUPS : (a + 5) * GROUPS]
        pc_ref[a] = (y * 128.0 + x).astype(I32)
        pc_ref[a + 4] = pltpu.roll(pc_ref[a], 64, 1)
    for a in range(3):
        pv_ref[a] = sorted_[(a + 8) * GROUPS : (a + 9) * GROUPS].astype(I32)
        pv_ref[a + 3] = pltpu.roll(pv_ref[a], 64, 1)


def sample_all(table, pc_ref, pv_ref, found):
    def sample(g, carry):
        for k in range(L // 8):
            swap = 0 if k < 5 else 1
            cols = [pc_ref[a + 4 * swap, pl.ds(g, 1), :] for a in range(4)]
            levs = [pv_ref[a + 3 * swap, pl.ds(g, 1), :] for a in range(3)]
            level = iota((8, 128), 0) + k * 8
            passed = [jnp.where(v <= level, 1, 0) for v in levs]
            element = passed[0] + passed[1] + passed[2]
            at = jnp.where(
                element < 2,
                jnp.where(element < 1, cols[0], cols[1]),
                jnp.where(element < 3, cols[2], cols[3]),
            )
            x, y = at & 127, at >> 7
            acc = jnp.zeros((8, 128), F32)
            for row in range(Y):
                got = jnp.take_along_axis(
                    table[row, k * 8 : k * 8 + 8, :], x, axis=1, mode="promise_in_bounds"
                )
                acc = jnp.where(y == row, got, acc)
            found[g, k * 8 : k * 8 + 8, :] = acc
        return carry

    lax.fori_loop(0, GROUPS, sample, 0)
    found[GROUPS] = jnp.zeros((L, 128), F32)


def first_kernel(
    v_hbm, f_hbm, r_ref, own_ref, col_ref, lev_ref, n_ref, s_ref, e_ref, w_ref,
    out_hbm, hi_hbm, lo_hbm, low_row, high_row, cols, found, start_ref, count_ref,
    v, f, out, hi, lo, table, adv, summed, pc, pv, place, v_sem, f_sem, o_sem, m_sem,
):
    levels = [pl.ds(b * BL, BL) for b in range(NB)]
    v_in = copies([(v_hbm.at[:, d], v.at[b]) for b, d in enumerate(levels)], v_sem)
    f_in = copies([(f_hbm.at[:, d], f.at[b]) for b, d in enumerate(levels)], f_sem)
    outs = copies([(out.at[b], out_hbm.at[:, d]) for b, d in enumerate(levels)], o_sem)
    made = copies([(hi, hi_hbm), (lo, lo_hbm)], m_sem)
    for b in range(NB):
        v_in[b].start()
        f_in[b].start()
    spread(r_ref, hi, lo)
    for c in made:
        c.start()
    order(own_ref, col_ref, lev_ref, pc, pv, start_ref, count_ref, place)
    for b in range(NB):
        v_in[b].wait()
        f_in[b].wait()
        here = levels[b]
        transport_block(
            adv, v.at[b], f.at[b], n_ref.at[:, here], s_ref.at[:, here], e_ref.at[b], w_ref.at[b]
        )
        for q in range(YT):
            parts = tiles(mixed(hi[b * YT + q], lo[b * YT + q], adv[q]))
            rows = pl.ds(q * 8, 8)
            for t in range(T):
                for j in range(BL):
                    out[b, t, j, rows, :] = parts[t][j]
                cols[b, t, rows, :] = edge_columns(parts[t])
            for j in range(BL):
                summed[pl.ds(j * Y + q * 8, 8), :] = parts[0][j] + parts[1][j] + parts[2][j]
        for y in range(Y):
            table[y, here, :] = summed[pl.ds(y, BL, stride=Y), :]
        for t in range(T):
            low_row[t, here, :] = out[b, t, :, 0, :]
            high_row[t, here, :] = out[b, t, :, Y - 1, :]
        outs[b].start()
    sample_all(table, pc, pv, found)
    for c in outs + made:
        c.wait()


def first_step(state, outflow, rows, owner, path_column, path_level, halo):
    vmem = lambda dims, dtype=F32: pltpu.VMEM(dims, dtype)
    return pl.pallas_call(
        first_kernel,
        in_specs=[ANY, ANY] + [IN_VMEM] * 8,
        out_specs=[ANY, ANY, ANY] + [IN_VMEM] * 6,
        out_shape=[
            shape((T, L, Y, X)),
            shape((NB * YT, K, K), BF16),
            shape((NB * YT, K, K), BF16),
            shape((T, L, X)),
            shape((T, L, X)),
            shape((NB, T, Y, X)),
            shape((GROUPS + 1, L, 128)),
            shape((1, OWN), I32),
            shape((1, OWN), I32),
        ],
        scratch_shapes=[
            vmem((NB, T, BL, Y, X)),
            vmem((NB, 4, BL, Y, X)),
            vmem((NB, T, BL, Y, X)),
            vmem((NB * YT, K, K), BF16),
            vmem((NB * YT, K, K), BF16),
            vmem((Y, L, X)),
            vmem((YT, K, T * X)),
            vmem((BL * Y, X)),
            vmem((8, GROUPS, 128), I32),
            vmem((6, GROUPS, 128), I32),
            vmem((1, SND), I32),
            pltpu.SemaphoreType.DMA((NB,)),
            pltpu.SemaphoreType.DMA((NB,)),
            pltpu.SemaphoreType.DMA((NB,)),
            pltpu.SemaphoreType.DMA((2,)),
        ],
        compiler_params=params(),
        name="first_step",
    )(state, outflow, rows, owner.reshape(1, SND), path_column.T, path_level.T, *halo)


def weigh_kernel(
    start_ref, count_ref, half_ref, found_hbm, k_hbm, out_ref, found, k, kept, found_sem, k_sem
):
    deep = OWN // PACKS
    k_in = copies([(k_hbm.at[pl.ds(c * deep, deep)], k.at[c]) for c in range(PACKS)], k_sem)
    (found_in,) = copies([(found_hbm, found)], found_sem)
    found_in.start()
    for c in k_in:
        c.start()
    found_in.wait()
    lane = iota((8, 128), 1)
    many = 8
    for c in range(PACKS):
        k_in[c].wait()

        def some(step, carry):
            sums = []
            for n in range(many):
                o = c * deep + step * many + n
                start, count = start_ref[0, o], count_ref[0, o]
                group, offset = jnp.minimum(start >> 7, GROUPS - 1), start & 127
                near = lane >= offset
                near_high = (lane ^ 64) >= offset
                low = ((lane - offset) & 127) < 64
                acc = jnp.zeros((8, 128), F32)
                for r in range(5):
                    rows = slice(r * 8, r * 8 + 8)
                    z = jnp.where(near, found[group, rows, :], found[group + 1, rows, :])
                    if r < 4:
                        high = slice((r + 5) * 8, (r + 6) * 8)
                        z_high = jnp.where(
                            near_high, found[group, high, :], found[group + 1, high, :]
                        )
                        z = jnp.where(low, z, z_high)
                    turned = pltpu.roll(z, (half_ref[0] + 128 - offset) & 127, 1)
                    acc = acc + turned * k[c, step * many + n, rows, :]
                sums.append(jnp.where((lane & 63) < count, acc, 0.0))
            for n in range(many):
                kept[pl.ds((c * deep + step * many + n) * 8, 8), :] = sums[n]
            return carry

        lax.fori_loop(0, deep // many, some, 0)
    total = kept[pl.ds(0, OWN, stride=8), :]
    for r in range(1, 8):
        total = total + kept[pl.ds(r, OWN, stride=8), :]
    out_ref[...] = total + pltpu.roll(total, 64, 1)


def weigh(start, count, half, found, arrived):
    return pl.pallas_call(
        weigh_kernel,
        in_specs=[IN_SMEM, IN_SMEM, IN_SMEM, ANY, ANY],
        out_specs=IN_VMEM,
        out_shape=shape((OWN, 128)),
        scratch_shapes=[
            pltpu.VMEM((GROUPS + 1, L, 128), F32),
            pltpu.VMEM((PACKS, OWN // PACKS, ROWS, 128), F32),
            pltpu.VMEM((OWN * 8, 128), F32),
            pltpu.SemaphoreType.DMA((1,)),
            pltpu.SemaphoreType.DMA((PACKS,)),
        ],
        compiler_params=params(),
        name="weigh",
    )(start, count, half, found, arrived)


def body(state, outflow, mix_blocks, owner, path_column, path_level, weights):
    axes = ("lon", "lat")
    *sides, packed = prepare(state, weights)
    packed, halo = lax.optimization_barrier((packed, exchange(*sides)))
    arrived = lax.all_to_all(packed, axes, 0, 0, tiled=True)
    rows = mix_blocks.reshape(YT, 8, NB, BL, BL).transpose(2, 0, 1, 4, 3).reshape(NB * YT, K, BL)
    half = (lax.axis_index("lat") % 2 * 64).astype(I32).reshape(1)
    first, hi, lo, *sides, found, start, count = first_step(
        state, outflow, rows, owner, path_column, path_level, halo
    )
    sums = weigh(start, count, half, found, arrived)
    sensitivity = lax.all_to_all(sums, axes, 0, 0, tiled=True)[:, :CAP]
    final = last_step(first, outflow, exchange(*sides), (hi, lo))
    return final, sensitivity.reshape(OWN * CAP)


def solution(mesh):
    return jax.shard_map(
        body,
        mesh=mesh,
        in_specs=(
            P(None, None, "lat", "lon"),
            P(None, None, "lat", "lon"),
            P("lat", None, None, None),
            P(("lon", "lat"), None),
            P(("lon", "lat"), None),
            P(("lon", "lat"), None),
            P(None, ("lon", "lat")),
        ),
        out_specs=(P(None, None, "lat", "lon"), P(("lon", "lat"))),
        check_vma=False,
    )
```

time: 114 us -> 100 us (0.88)
  Pallas kernels: 57.9 us -> 49.1 us
  waiting for transfers between devices: 10.5 us -> 2.64 us
  starting transfers between devices: 40.2 us -> 43.1 us
    ppermute x4, waiting for transfers between devices: 10.4 us -> 0.01 us  [the longest x2 0.01 us: exchange(): from_west = lax.ppermute(cols, 'lon', east)]
    pallas_call x8 -> x4, Pallas kernels: 57.9 us -> 49.1 us  [the longest x1 29.6 us: first_step(): pl.pallas_call(first_kernel, in_specs=[ANY, ANY] + [IN_VMEM] * 8, out_spe...]
    all_to_all x1, starting transfers between devices: 6.96 us -> 11.8 us  [body(): arrived = lax.all_to_all(packed, axes, 0, 0, tiled=True)]
    all_to_all x1, starting transfers between devices: 10.6 us -> 8.31 us  [body(): sensitivity = lax.all_to_all(sums, axes, 0, 0, tiled=True)[:, :CAP]]
    ppermute x2, waiting for transfers between devices: 0.01 us -> 1.63 us  [exchange(): south = lax.ppermute(high_row, 'lat', up)]
  transfers between devices with their start and end apart: 10 -> 10, of which waited for: 3 -> 2; matrix products, arithmetic and copies ran while one was open for 1% -> 1% of each run, Pallas kernels for 47% -> 44%
where the time goes in v1:
time: 100 us; the launch traced here: 99.3 us
  Pallas kernels  49.1 us (49%)
  starting transfers between devices  43.1 us (43%)
  local copies, waits for them, and re-layouts  3.57 us (4%)
  waiting for transfers between devices  2.64 us (3%)
    pallas_call x1, Pallas kernels, first_step(): pl.pallas_call(first_kernel, in_specs=[ANY, ANY] + [IN_VMEM] * 8, out_spe...  29.6 us
    all_to_all x1, starting transfers between devices, body(): arrived = lax.all_to_all(packed, axes, 0, 0, tiled=True)  11.8 us
    ppermute x2, starting transfers between devices, exchange(): from_east = lax.ppermute(cols, 'lon', west)  11.3 us
    ppermute x2, starting transfers between devices, exchange(): south = lax.ppermute(high_row, 'lat', up)  9.1 us
    pallas_call x1, Pallas kernels, last_step(): pl.pallas_call(last_kernel, grid=(NB,), in_specs=[pl.BlockSpec((T, BL, Y,...  8.75 us
    all_to_all x1, starting transfers between devices, body(): sensitivity = lax.all_to_all(sums, axes, 0, 0, tiled=True)[:, :CAP]  8.31 us
    pallas_call x1, Pallas kernels, prepare(): pl.pallas_call(prepare_kernel, in_specs=[ANY, ANY], out_specs=[IN_VMEM, I...  5.4 us
    pallas_call x1, Pallas kernels, weigh(): pl.pallas_call(weigh_kernel, in_specs=[IN_SMEM, IN_SMEM, IN_SMEM, ANY, AN...  5.37 us
  transfers between devices with their start and end apart: 10, of which 2 were waited for; matrix products, arithmetic and copies ran while one was open for 1% of the time, Pallas kernels for 44%

profile of v1, /device:TPU:0, one launch (start us, length us, event | category | flops | bytes accessed | tf_op | source)
XLA Modules:
  0.0 99.3 jit_solution(1390068616642776923)
XLA Ops:
  0.6 5.4 %prepare.1 = (f32[3,72,128]{2,1,0:T(8,128)}, f32[3,72,128]{2,1,0:T(8,128)}, f32[3,3,32,128]{3,2,1,0:T(8,128)}, f32[128,40,128]{2,1,0:T(8,128)}) custom-call(f32[3,2304,128]{2,1,0:T(8,128)} %bitcast.15, f32[72,8192]{1,0:T(8,128)} %k_hbm.1), custom_call_target="tpu_custom_call" | custom-call | tf_op jit(solution)/shard_map/prepare/pallas_call | solution.py:86
  6.0 0.1 collective-permute-start.3
  6.1 5.9 %collective-permute-start.2 = (f32[3,3,32,128]{3,2,1,0:T(8,128)}, f32[3,3,32,128]{3,2,1,0:T(8,128)S(1)}, u32[]{:S(2)}, u32[]{:S(2)}) collective-permute-start(f32[3,3,32,128]{3,2,1,0:T(8,128)} %get-tuple-element.23), channel_id=1, source_target_pairs={{8,0},{16,8},{24,16},{32,24},{40,32},{48,40},{56,48},{64,56},{72,6... | collective-permute-start | bytes 442376 | tf_op jit(solution)/shard_map/ppermute | solution.py:117
  12.0 1.3 %collective-permute-start = (f32[3,72,128]{2,1,0:T(8,128)}, f32[3,72,128]{2,1,0:T(8,128)S(1)}, u32[]{:S(2)}, u32[]{:S(2)}) collective-permute-start(f32[3,72,128]{2,1,0:T(8,128)} %get-tuple-element.21), channel_id=1, source_target_pairs={{1,0},{2,1},{3,2},{4,3},{5,4},{6,5},{7,6},{9,8},{10,9},{11,10},{12... | collective-permute-start | bytes 331784 | tf_op jit(solution)/shard_map/ppermute | solution.py:115
  13.3 4.6 %collective-permute-start.1 = (f32[3,72,128]{2,1,0:T(8,128)}, f32[3,72,128]{2,1,0:T(8,128)S(1)}, u32[]{:S(2)}, u32[]{:S(2)}) collective-permute-start(f32[3,72,128]{2,1,0:T(8,128)} %get-tuple-element.22), channel_id=1, source_target_pairs={{0,1},{1,2},{2,3},{3,4},{4,5},{5,6},{6,7},{8,9},{9,10},{10,11},{11... | collective-permute-start | bytes 331784 | tf_op jit(solution)/shard_map/ppermute | solution.py:116
  17.9 1.0 collective-permute-done.n_ref
  18.9 0.0 copy-start.7
  18.9 1.6 %collective-permute-done.1.s_ref = f32[3,72,128]{2,1,0:T(8,128)S(1)} collective-permute-done((f32[3,72,128]{2,1,0:T(8,128)}, f32[3,72,128]{2,1,0:T(8,128)S(1)}, u32[]{:S(2)}, u32[]{:S(2)}) %collective-permute-start.1) | collective-permute-done | bytes 110624 | tf_op jit(solution)/shard_map/ppermute | solution.py:116
  20.5 0.0 copy-start.8
  20.5 0.0 collective-permute-done.3.w_ref
  20.5 0.0 copy-start.1
  20.5 0.0 collective-permute-done.2.e_ref
  20.5 0.0 copy-start.2
  20.5 0.0 copy-start
  20.5 0.0 copy-done.7
  20.5 0.6 copy-done.8
  21.1 0.1 copy-done.1
  21.2 0.1 copy-done.2
  21.3 11.8 %all-to-all-start = ((f32[128,40,128]{2,1,0:T(8,128)}), f32[128,40,128]{2,1,0:T(8,128)}, u32[]{:S(2)}, u32[]{:S(2)}) async-start(f32[128,40,128]{2,1,0:T(8,128)} %get-tuple-element.37), calls=%async_computation | async-start | bytes 5242880 | tf_op jit(solution)/shard_map/all_to_all | solution.py:445
  33.0 0.0 copy-done
  33.0 1.4 %copy.15 = f32[32,3,24,24]{2,3,0,1:T(8,128)} copy(f32[32,3,24,24]{0,3,2,1:T(8,128)S(1)} %copy-done) | data formatting | bytes 442368 | tf_op jit(solution)/shard_map/transpose | solution.py:446
  34.5 29.6 %first_step.1 = (f32[3,72,32,128]{3,2,1,0:T(8,128)}, bf16[12,192,192]{2,1,0:T(8,128)(2,1)}, bf16[12,192,192]{2,1,0:T(8,128)(2,1)}, f32[3,72,128]{2,1,0:T(8,128)}...) custom-call(f32[3,72,32,128]{3,2,1,0:T(8,128)} %v_hbm.1, ...), custom_call_target="tpu_custom_call" | custom-call | tf_op jit(solution)/shard_map/first_step/pallas_call | solution.py:338
  64.1 0.1 collective-permute-start.7
  64.2 5.3 %collective-permute-start.6 = (f32[3,3,32,128]{3,2,1,0:T(8,128)}, f32[3,3,32,128]{3,2,1,0:T(8,128)S(1)}, u32[]{:S(2)}, u32[]{:S(2)}) collective-permute-start(f32[3,3,32,128]{3,2,1,0:T(8,128)} %get-tuple-element.31), channel_id=1, source_target_pairs={{8,0},{16,8},{24,16},{32,24},{40,32},{48,40},{56,48},{64,56},{72,6... | collective-permute-start | bytes 442376 | tf_op jit(solution)/shard_map/ppermute | solution.py:117
  69.5 1.3 %collective-permute-start.4 = (f32[3,72,128]{2,1,0:T(8,128)}, f32[3,72,128]{2,1,0:T(8,128)S(1)}, u32[]{:S(2)}, u32[]{:S(2)}) collective-permute-start(f32[3,72,128]{2,1,0:T(8,128)} %get-tuple-element.29), channel_id=1, source_target_pairs={{1,0},{2,1},{3,2},{4,3},{5,4},{6,5},{7,6},{9,8},{10,9},{11,10},{12... | collective-permute-start | bytes 331784 | tf_op jit(solution)/shard_map/ppermute | solution.py:115
  70.8 4.6 %collective-permute-start.5 = (f32[3,72,128]{2,1,0:T(8,128)}, f32[3,72,128]{2,1,0:T(8,128)S(1)}, u32[]{:S(2)}, u32[]{:S(2)}) collective-permute-start(f32[3,72,128]{2,1,0:T(8,128)} %get-tuple-element.30), channel_id=1, source_target_pairs={{0,1},{1,2},{2,3},{3,4},{4,5},{5,6},{6,7},{8,9},{9,10},{10,11},{11... | collective-permute-start | bytes 331784 | tf_op jit(solution)/shard_map/ppermute | solution.py:116
  75.4 0.0 all-to-all-done.k_hbm
  75.4 5.4 %weigh.1 = f32[128,128]{1,0:T(8,128)} custom-call(s32[1,128]{1,0:T(1,128)} %get-tuple-element.34.start_ref, s32[1,128]{1,0:T(1,128)} %get-tuple-element.35.count_ref, s32[1]{0:T(128)} %bitcast.8.half_ref, f32[33,72,128]{2,1,0:T(8,128)} %get-tuple-element.36.found_hbm, f32[128,40,128]{2,1,0:T(8,128)} %all-to-all-done.k_hbm), custom_call_target="tpu_custom_call" | custom-call | tf_op jit(solution)/shard_map/weigh/pallas_call | solution.py:424
  80.8 8.3 %all-to-all-start.1 = ((f32[128,1,128]{2,1,0:T(1,128)}), f32[128,1,128]{2,1,0:T(1,128)S(1)}, u32[]{:S(2)}, u32[]{:S(2)}) async-start(f32[128,1,128]{2,1,0:T(1,128)} %bitcast.17), calls=%async_computation.1 | async-start | bytes 131072 | tf_op jit(solution)/shard_map/all_to_all | solution.py:452
  89.1 0.0 collective-permute-done.4.n_ref
  89.1 0.0 copy-start.5
  89.1 0.0 collective-permute-done.5.s_ref
  89.1 0.0 copy-start.6
  89.1 0.0 collective-permute-done.7.w_ref
  89.1 0.0 copy-start.3
  89.2 0.0 collective-permute-done.6.e_ref
  89.2 0.0 copy-start.4
  89.2 0.6 copy-done.5
  89.7 0.1 copy-done.6
  89.8 0.1 copy-done.3
  89.8 0.1 copy-done.4
  89.9 8.7 %last_step.1 = f32[3,72,32,128]{3,2,1,0:T(8,128)} custom-call(f32[3,72,32,128]{3,2,1,0:T(8,128)} %get-tuple-element.28.v_ref, f32[4,72,32,128]{3,2,1,0:T(8,128)} %f_ref.1, f32[3,72,128]{2,1,0:T(8,128)} %copy-done.5, f32[3,72,128]{2,1,0:T(8,128)} %copy-done.6, f32[3,3,32,128]{3,2,1,0:T(8,128)} %copy-done.4, f32[3,3,32,128]{3,2,1,0:T(8,128)} %copy-done.3, ...), custom_call_target="tpu_custom_call" | custom-call | tf_op jit(solution)/shard_map/last_step/pallas_call | solution.py:182
  98.6 0.0 all-to-all-done.1
  98.7 0.7 reshape.29
Async XLA Ops:
  6.0 14.5 %collective-permute-start.3 = (f32[3,3,32,128]{3,2,1,0:T(8,128)}, f32[3,3,32,128]{3,2,1,0:T(8,128)S(1)}, u32[]{:S(2)}, u32[]{:S(2)}) collective-permute-start(f32[3,3,32,128]{3,2,1,0:T(8,128)} %get-tuple-element.23), channel_id=1, source_target_pairs={{0,8},{8,16},{16,24},{24,32},{32,40},{40,48},{48,56},{56,64},{64,7... | collective-permute-start | bytes 442376 | tf_op jit(solution)/shard_map/ppermute | solution.py:118
  6.1 14.4 %collective-permute-start.2 = (f32[3,3,32,128]{3,2,1,0:T(8,128)}, f32[3,3,32,128]{3,2,1,0:T(8,128)S(1)}, u32[]{:S(2)}, u32[]{:S(2)}) collective-permute-start(f32[3,3,32,128]{3,2,1,0:T(8,128)} %get-tuple-element.23), channel_id=1, source_target_pairs={{8,0},{16,8},{24,16},{32,24},{40,32},{48,40},{56,48},{64,56},{72,6... | collective-permute-start | bytes 442376 | tf_op jit(solution)/shard_map/ppermute | solution.py:117
  12.0 6.8 %collective-permute-start = (f32[3,72,128]{2,1,0:T(8,128)}, f32[3,72,128]{2,1,0:T(8,128)S(1)}, u32[]{:S(2)}, u32[]{:S(2)}) collective-permute-start(f32[3,72,128]{2,1,0:T(8,128)} %get-tuple-element.21), channel_id=1, source_target_pairs={{1,0},{2,1},{3,2},{4,3},{5,4},{6,5},{7,6},{9,8},{10,9},{11,10},{12... | collective-permute-start | bytes 331784 | tf_op jit(solution)/shard_map/ppermute | solution.py:115
  13.3 7.2 %collective-permute-start.1 = (f32[3,72,128]{2,1,0:T(8,128)}, f32[3,72,128]{2,1,0:T(8,128)S(1)}, u32[]{:S(2)}, u32[]{:S(2)}) collective-permute-start(f32[3,72,128]{2,1,0:T(8,128)} %get-tuple-element.22), channel_id=1, source_target_pairs={{0,1},{1,2},{2,3},{3,4},{4,5},{5,6},{6,7},{8,9},{9,10},{10,11},{11... | collective-permute-start | bytes 331784 | tf_op jit(solution)/shard_map/ppermute | solution.py:116
  18.9 1.7 %copy-start.7 = (f32[3,72,128]{2,1,0:T(8,128)}, f32[3,72,128]{2,1,0:T(8,128)S(1)}, u32[]{:S(2)}) copy-start(f32[3,72,128]{2,1,0:T(8,128)S(1)} %collective-permute-done.n_ref) | copy-start | bytes 331780
  20.5 0.6 copy-start.8
  20.5 0.7 copy-start.1
  20.5 0.7 copy-start.2
  20.5 12.5 %copy-start = (f32[32,3,24,24]{0,3,2,1:T(8,128)S(1)}, f32[32,3,24,24]{0,3,2,1:T(8,128)}, u32[]{:S(2)}) copy-start(f32[32,3,24,24]{0,3,2,1:T(8,128)} %param.9) | copy-start | bytes 663556
  21.3 54.1 %all-to-all-start = ((f32[128,40,128]{2,1,0:T(8,128)}), f32[128,40,128]{2,1,0:T(8,128)}, u32[]{:S(2)}, u32[]{:S(2)}) async-start(f32[128,40,128]{2,1,0:T(8,128)} %get-tuple-element.37), calls=%async_computation | async-start | bytes 5242880 | tf_op jit(solution)/shard_map/all_to_all | solution.py:445
  64.1 25.0 %collective-permute-start.7 = (f32[3,3,32,128]{3,2,1,0:T(8,128)}, f32[3,3,32,128]{3,2,1,0:T(8,128)S(1)}, u32[]{:S(2)}, u32[]{:S(2)}) collective-permute-start(f32[3,3,32,128]{3,2,1,0:T(8,128)} %get-tuple-element.31), channel_id=1, source_target_pairs={{0,8},{8,16},{16,24},{24,32},{32,40},{40,48},{48,56},{56,64},{64,7... | collective-permute-start | bytes 442376 | tf_op jit(solution)/shard_map/ppermute | solution.py:118
  64.2 25.0 %collective-permute-start.6 = (f32[3,3,32,128]{3,2,1,0:T(8,128)}, f32[3,3,32,128]{3,2,1,0:T(8,128)S(1)}, u32[]{:S(2)}, u32[]{:S(2)}) collective-permute-start(f32[3,3,32,128]{3,2,1,0:T(8,128)} %get-tuple-element.31), channel_id=1, source_target_pairs={{8,0},{16,8},{24,16},{32,24},{40,32},{48,40},{56,48},{64,56},{72,6... | collective-permute-start | bytes 442376 | tf_op jit(solution)/shard_map/ppermute | solution.py:117
  69.5 19.6 %collective-permute-start.4 = (f32[3,72,128]{2,1,0:T(8,128)}, f32[3,72,128]{2,1,0:T(8,128)S(1)}, u32[]{:S(2)}, u32[]{:S(2)}) collective-permute-start(f32[3,72,128]{2,1,0:T(8,128)} %get-tuple-element.29), channel_id=1, source_target_pairs={{1,0},{2,1},{3,2},{4,3},{5,4},{6,5},{7,6},{9,8},{10,9},{11,10},{12... | collective-permute-start | bytes 331784 | tf_op jit(solution)/shard_map/ppermute | solution.py:115
  70.8 18.3 %collective-permute-start.5 = (f32[3,72,128]{2,1,0:T(8,128)}, f32[3,72,128]{2,1,0:T(8,128)S(1)}, u32[]{:S(2)}, u32[]{:S(2)}) collective-permute-start(f32[3,72,128]{2,1,0:T(8,128)} %get-tuple-element.30), channel_id=1, source_target_pairs={{0,1},{1,2},{2,3},{3,4},{4,5},{5,6},{6,7},{8,9},{9,10},{10,11},{11... | collective-permute-start | bytes 331784 | tf_op jit(solution)/shard_map/ppermute | solution.py:116
  80.8 17.9 %all-to-all-start.1 = ((f32[128,1,128]{2,1,0:T(1,128)}), f32[128,1,128]{2,1,0:T(1,128)S(1)}, u32[]{:S(2)}, u32[]{:S(2)}) async-start(f32[128,1,128]{2,1,0:T(1,128)} %bitcast.17), calls=%async_computation.1 | async-start | bytes 131072 | tf_op jit(solution)/shard_map/all_to_all | solution.py:452
  89.1 0.6 copy-start.5
  89.1 0.7 copy-start.6
  89.1 0.7 copy-start.3
  89.2 0.7 copy-start.4

commit v2 on v1

--- a/solution.py
+++ b/solution.py
@@ -319,7 +319,6 @@
             for t in range(T):
                 for j in range(BL):
                     out[b, t, j, rows, :] = parts[t][j]
-                cols[b, t, rows, :] = edge_columns(parts[t])
             for j in range(BL):
                 summed[pl.ds(j * Y + q * 8, 8), :] = parts[0][j] + parts[1][j] + parts[2][j]
         for y in range(Y):
@@ -328,6 +327,18 @@
             low_row[t, here, :] = out[b, t, :, 0, :]
             high_row[t, here, :] = out[b, t, :, Y - 1, :]
         outs[b].start()
+    lane = iota((Y, X), 1)
+
+    def columns(i, both):
+        here = lane >> 1 == i
+        return tuple(
+            jnp.where(here, pltpu.roll(out[n // T, n % T, i], 2 * i + 1, 1), both[n])
+            for n in range(NB * T)
+        )
+
+    both = lax.fori_loop(0, BL, columns, (jnp.zeros((Y, X), F32),) * (NB * T))
+    for n in range(NB * T):
+        cols[n // T, n % T] = both[n]
     sample_all(table, pc, pv, found)
     for c in outs + made:
         c.wait()
@@ -383,7 +394,7 @@
         c.start()
     found_in.wait()
     lane = iota((8, 128), 1)
-    many = 8
+    many = 16
     for c in range(PACKS):
         k_in[c].wait()
 

time: 100 us -> 98.4 us (0.984)
  Pallas kernels: 49.1 us -> 47.4 us
    pallas_call x1, Pallas kernels: 29.6 us -> 28.5 us  [first_step(): pl.pallas_call(first_kernel, in_specs=[ANY, ANY] + [IN_VMEM] * 8, out_spe...]
  transfers between devices with their start and end apart: 10 -> 10, of which waited for: 2 -> 2; matrix products, arithmetic and copies ran while one was open for 1% -> 1% of each run, Pallas kernels for 44% -> 43%
where the time goes in v2:
time: 98.4 us; the launch traced here: 97.6 us
  Pallas kernels  47.4 us (48%)
  starting transfers between devices  43.1 us (44%)
  local copies, waits for them, and re-layouts  3.57 us (4%)
  waiting for transfers between devices  2.64 us (3%)
    pallas_call x1, Pallas kernels, first_step(): pl.pallas_call(first_kernel, in_specs=[ANY, ANY] + [IN_VMEM] * 8, out_spe...  28.5 us
    all_to_all x1, starting transfers between devices, body(): arrived = lax.all_to_all(packed, axes, 0, 0, tiled=True)  11.8 us
    ppermute x2, starting transfers between devices, exchange(): from_east = lax.ppermute(cols, 'lon', west)  11.3 us
    ppermute x2, starting transfers between devices, exchange(): south = lax.ppermute(high_row, 'lat', up)  9.1 us
    pallas_call x1, Pallas kernels, last_step(): pl.pallas_call(last_kernel, grid=(NB,), in_specs=[pl.BlockSpec((T, BL, Y,...  8.74 us
    all_to_all x1, starting transfers between devices, body(): sensitivity = lax.all_to_all(sums, axes, 0, 0, tiled=True)[:, :CAP]  8.3 us
    pallas_call x1, Pallas kernels, prepare(): pl.pallas_call(prepare_kernel, in_specs=[ANY, ANY], out_specs=[IN_VMEM, I...  5.4 us
    pallas_call x1, Pallas kernels, weigh(): pl.pallas_call(weigh_kernel, in_specs=[IN_SMEM, IN_SMEM, IN_SMEM, ANY, AN...  4.7 us
  transfers between devices with their start and end apart: 10, of which 2 were waited for; matrix products, arithmetic and copies ran while one was open for 1% of the time, Pallas kernels for 43%

profile of v2, /device:TPU:0, one launch (start us, length us, event | category | flops | bytes accessed | tf_op | source)
XLA Modules:
  0.0 97.6 jit_solution(15356913170269171513)
XLA Ops:
  0.6 5.4 %prepare.1 = (f32[3,72,128]{2,1,0:T(8,128)}, f32[3,72,128]{2,1,0:T(8,128)}, f32[3,3,32,128]{3,2,1,0:T(8,128)}, f32[128,40,128]{2,1,0:T(8,128)}) custom-call(f32[3,2304,128]{2,1,0:T(8,128)} %bitcast.15, f32[72,8192]{1,0:T(8,128)} %k_hbm.1), custom_call_target="tpu_custom_call" | custom-call | tf_op jit(solution)/shard_map/prepare/pallas_call | solution.py:86
  6.0 0.1 collective-permute-start.3
  6.1 5.9 %collective-permute-start.2 = (f32[3,3,32,128]{3,2,1,0:T(8,128)}, f32[3,3,32,128]{3,2,1,0:T(8,128)S(1)}, u32[]{:S(2)}, u32[]{:S(2)}) collective-permute-start(f32[3,3,32,128]{3,2,1,0:T(8,128)} %get-tuple-element.23), channel_id=1, source_target_pairs={{8,0},{16,8},{24,16},{32,24},{40,32},{48,40},{56,48},{64,56},{72,6... | collective-permute-start | bytes 442376 | tf_op jit(solution)/shard_map/ppermute | solution.py:117
  12.0 1.3 %collective-permute-start = (f32[3,72,128]{2,1,0:T(8,128)}, f32[3,72,128]{2,1,0:T(8,128)S(1)}, u32[]{:S(2)}, u32[]{:S(2)}) collective-permute-start(f32[3,72,128]{2,1,0:T(8,128)} %get-tuple-element.21), channel_id=1, source_target_pairs={{1,0},{2,1},{3,2},{4,3},{5,4},{6,5},{7,6},{9,8},{10,9},{11,10},{12... | collective-permute-start | bytes 331784 | tf_op jit(solution)/shard_map/ppermute | solution.py:115
  13.3 4.6 %collective-permute-start.1 = (f32[3,72,128]{2,1,0:T(8,128)}, f32[3,72,128]{2,1,0:T(8,128)S(1)}, u32[]{:S(2)}, u32[]{:S(2)}) collective-permute-start(f32[3,72,128]{2,1,0:T(8,128)} %get-tuple-element.22), channel_id=1, source_target_pairs={{0,1},{1,2},{2,3},{3,4},{4,5},{5,6},{6,7},{8,9},{9,10},{10,11},{11... | collective-permute-start | bytes 331784 | tf_op jit(solution)/shard_map/ppermute | solution.py:116
  17.9 1.0 %collective-permute-done.n_ref = f32[3,72,128]{2,1,0:T(8,128)S(1)} collective-permute-done((f32[3,72,128]{2,1,0:T(8,128)}, f32[3,72,128]{2,1,0:T(8,128)S(1)}, u32[]{:S(2)}, u32[]{:S(2)}) %collective-permute-start) | collective-permute-done | bytes 110624 | tf_op jit(solution)/shard_map/ppermute | solution.py:115
  18.9 0.0 copy-start.7
  18.9 1.6 %collective-permute-done.1.s_ref = f32[3,72,128]{2,1,0:T(8,128)S(1)} collective-permute-done((f32[3,72,128]{2,1,0:T(8,128)}, f32[3,72,128]{2,1,0:T(8,128)S(1)}, u32[]{:S(2)}, u32[]{:S(2)}) %collective-permute-start.1) | collective-permute-done | bytes 110624 | tf_op jit(solution)/shard_map/ppermute | solution.py:116
  20.5 0.0 copy-start.8
  20.5 0.0 collective-permute-done.3.w_ref
  20.5 0.0 copy-start.1
  20.5 0.0 collective-permute-done.2.e_ref
  20.5 0.0 copy-start.2
  20.5 0.0 copy-start
  20.5 0.0 copy-done.7
  20.5 0.6 copy-done.8
  21.1 0.1 copy-done.1
  21.2 0.1 copy-done.2
  21.3 11.8 %all-to-all-start = ((f32[128,40,128]{2,1,0:T(8,128)}), f32[128,40,128]{2,1,0:T(8,128)}, u32[]{:S(2)}, u32[]{:S(2)}) async-start(f32[128,40,128]{2,1,0:T(8,128)} %get-tuple-element.37), calls=%async_computation | async-start | bytes 5242880 | tf_op jit(solution)/shard_map/all_to_all | solution.py:456
  33.0 0.0 copy-done
  33.0 1.4 %copy.15 = f32[32,3,24,24]{2,3,0,1:T(8,128)} copy(f32[32,3,24,24]{0,3,2,1:T(8,128)S(1)} %copy-done) | data formatting | bytes 442368 | tf_op jit(solution)/shard_map/transpose | solution.py:457
  34.5 28.5 %first_step.1 = (f32[3,72,32,128]{3,2,1,0:T(8,128)}, bf16[12,192,192]{2,1,0:T(8,128)(2,1)}, bf16[12,192,192]{2,1,0:T(8,128)(2,1)}, f32[3,72,128]{2,1,0:T(8,128)}...) custom-call(f32[3,72,32,128]{3,2,1,0:T(8,128)} %v_hbm.1, ...), custom_call_target="tpu_custom_call" | custom-call | tf_op jit(solution)/shard_map/first_step/pallas_call | solution.py:349
  63.0 0.1 collective-permute-start.7
  63.1 5.3 %collective-permute-start.6 = (f32[3,3,32,128]{3,2,1,0:T(8,128)}, f32[3,3,32,128]{3,2,1,0:T(8,128)S(1)}, u32[]{:S(2)}, u32[]{:S(2)}) collective-permute-start(f32[3,3,32,128]{3,2,1,0:T(8,128)} %get-tuple-element.31), channel_id=1, source_target_pairs={{8,0},{16,8},{24,16},{32,24},{40,32},{48,40},{56,48},{64,56},{72,6... | collective-permute-start | bytes 442376 | tf_op jit(solution)/shard_map/ppermute | solution.py:117
  68.4 1.3 %collective-permute-start.4 = (f32[3,72,128]{2,1,0:T(8,128)}, f32[3,72,128]{2,1,0:T(8,128)S(1)}, u32[]{:S(2)}, u32[]{:S(2)}) collective-permute-start(f32[3,72,128]{2,1,0:T(8,128)} %get-tuple-element.29), channel_id=1, source_target_pairs={{1,0},{2,1},{3,2},{4,3},{5,4},{6,5},{7,6},{9,8},{10,9},{11,10},{12... | collective-permute-start | bytes 331784 | tf_op jit(solution)/shard_map/ppermute | solution.py:115
  69.7 4.6 %collective-permute-start.5 = (f32[3,72,128]{2,1,0:T(8,128)}, f32[3,72,128]{2,1,0:T(8,128)S(1)}, u32[]{:S(2)}, u32[]{:S(2)}) collective-permute-start(f32[3,72,128]{2,1,0:T(8,128)} %get-tuple-element.30), channel_id=1, source_target_pairs={{0,1},{1,2},{2,3},{3,4},{4,5},{5,6},{6,7},{8,9},{9,10},{10,11},{11... | collective-permute-start | bytes 331784 | tf_op jit(solution)/shard_map/ppermute | solution.py:116
  74.3 0.0 all-to-all-done.k_hbm
  74.3 4.7 %weigh.1 = f32[128,128]{1,0:T(8,128)} custom-call(s32[1,128]{1,0:T(1,128)} %get-tuple-element.34.start_ref, s32[1,128]{1,0:T(1,128)} %get-tuple-element.35.count_ref, s32[1]{0:T(128)} %bitcast.8.half_ref, f32[33,72,128]{2,1,0:T(8,128)} %get-tuple-element.36.found_hbm, f32[128,40,128]{2,1,0:T(8,128)} %all-to-all-done.k_hbm), custom_call_target="tpu_custom_call" | custom-call | tf_op jit(solution)/shard_map/weigh/pallas_call | solution.py:435
  79.0 8.3 %all-to-all-start.1 = ((f32[128,1,128]{2,1,0:T(1,128)}), f32[128,1,128]{2,1,0:T(1,128)S(1)}, u32[]{:S(2)}, u32[]{:S(2)}) async-start(f32[128,1,128]{2,1,0:T(1,128)} %bitcast.17), calls=%async_computation.1 | async-start | bytes 131072 | tf_op jit(solution)/shard_map/all_to_all | solution.py:463
  87.3 0.0 collective-permute-done.4.n_ref
  87.3 0.0 copy-start.5
  87.3 0.0 collective-permute-done.5.s_ref
  87.3 0.0 copy-start.6
  87.4 0.0 collective-permute-done.7.w_ref
  87.4 0.0 copy-start.3
  87.4 0.0 collective-permute-done.6.e_ref
  87.4 0.0 copy-start.4
  87.4 0.6 copy-done.5
  88.0 0.1 copy-done.6
  88.0 0.1 copy-done.3
  88.1 0.1 copy-done.4
  88.1 8.7 %last_step.1 = f32[3,72,32,128]{3,2,1,0:T(8,128)} custom-call(f32[3,72,32,128]{3,2,1,0:T(8,128)} %get-tuple-element.28.v_ref, f32[4,72,32,128]{3,2,1,0:T(8,128)} %f_ref.1, f32[3,72,128]{2,1,0:T(8,128)} %copy-done.5, f32[3,72,128]{2,1,0:T(8,128)} %copy-done.6, f32[3,3,32,128]{3,2,1,0:T(8,128)} %copy-done.4, f32[3,3,32,128]{3,2,1,0:T(8,128)} %copy-done.3, ...), custom_call_target="tpu_custom_call" | custom-call | tf_op jit(solution)/shard_map/last_step/pallas_call | solution.py:182
  96.9 0.0 all-to-all-done.1
  96.9 0.7 reshape.29
Async XLA Ops:
  6.0 14.5 %collective-permute-start.3 = (f32[3,3,32,128]{3,2,1,0:T(8,128)}, f32[3,3,32,128]{3,2,1,0:T(8,128)S(1)}, u32[]{:S(2)}, u32[]{:S(2)}) collective-permute-start(f32[3,3,32,128]{3,2,1,0:T(8,128)} %get-tuple-element.23), channel_id=1, source_target_pairs={{0,8},{8,16},{16,24},{24,32},{32,40},{40,48},{48,56},{56,64},{64,7... | collective-permute-start | bytes 442376 | tf_op jit(solution)/shard_map/ppermute | solution.py:118
  6.1 14.4 %collective-permute-start.2 = (f32[3,3,32,128]{3,2,1,0:T(8,128)}, f32[3,3,32,128]{3,2,1,0:T(8,128)S(1)}, u32[]{:S(2)}, u32[]{:S(2)}) collective-permute-start(f32[3,3,32,128]{3,2,1,0:T(8,128)} %get-tuple-element.23), channel_id=1, source_target_pairs={{8,0},{16,8},{24,16},{32,24},{40,32},{48,40},{56,48},{64,56},{72,6... | collective-permute-start | bytes 442376 | tf_op jit(solution)/shard_map/ppermute | solution.py:117
  12.0 6.8 %collective-permute-start = (f32[3,72,128]{2,1,0:T(8,128)}, f32[3,72,128]{2,1,0:T(8,128)S(1)}, u32[]{:S(2)}, u32[]{:S(2)}) collective-permute-start(f32[3,72,128]{2,1,0:T(8,128)} %get-tuple-element.21), channel_id=1, source_target_pairs={{1,0},{2,1},{3,2},{4,3},{5,4},{6,5},{7,6},{9,8},{10,9},{11,10},{12... | collective-permute-start | bytes 331784 | tf_op jit(solution)/shard_map/ppermute | solution.py:115
  13.3 7.2 %collective-permute-start.1 = (f32[3,72,128]{2,1,0:T(8,128)}, f32[3,72,128]{2,1,0:T(8,128)S(1)}, u32[]{:S(2)}, u32[]{:S(2)}) collective-permute-start(f32[3,72,128]{2,1,0:T(8,128)} %get-tuple-element.22), channel_id=1, source_target_pairs={{0,1},{1,2},{2,3},{3,4},{4,5},{5,6},{6,7},{8,9},{9,10},{10,11},{11... | collective-permute-start | bytes 331784 | tf_op jit(solution)/shard_map/ppermute | solution.py:116
  18.9 1.7 %copy-start.7 = (f32[3,72,128]{2,1,0:T(8,128)}, f32[3,72,128]{2,1,0:T(8,128)S(1)}, u32[]{:S(2)}) copy-start(f32[3,72,128]{2,1,0:T(8,128)S(1)} %collective-permute-done.n_ref) | copy-start | bytes 331780
  20.5 0.6 copy-start.8
  20.5 0.7 copy-start.1
  20.5 0.7 copy-start.2
  20.5 12.5 %copy-start = (f32[32,3,24,24]{0,3,2,1:T(8,128)S(1)}, f32[32,3,24,24]{0,3,2,1:T(8,128)}, u32[]{:S(2)}) copy-start(f32[32,3,24,24]{0,3,2,1:T(8,128)} %param.9) | copy-start | bytes 663556
  21.3 53.0 %all-to-all-start = ((f32[128,40,128]{2,1,0:T(8,128)}), f32[128,40,128]{2,1,0:T(8,128)}, u32[]{:S(2)}, u32[]{:S(2)}) async-start(f32[128,40,128]{2,1,0:T(8,128)} %get-tuple-element.37), calls=%async_computation | async-start | bytes 5242880 | tf_op jit(solution)/shard_map/all_to_all | solution.py:456
  63.0 24.4 %collective-permute-start.7 = (f32[3,3,32,128]{3,2,1,0:T(8,128)}, f32[3,3,32,128]{3,2,1,0:T(8,128)S(1)}, u32[]{:S(2)}, u32[]{:S(2)}) collective-permute-start(f32[3,3,32,128]{3,2,1,0:T(8,128)} %get-tuple-element.31), channel_id=1, source_target_pairs={{0,8},{8,16},{16,24},{24,32},{32,40},{40,48},{48,56},{56,64},{64,7... | collective-permute-start | bytes 442376 | tf_op jit(solution)/shard_map/ppermute | solution.py:118
  63.1 24.3 %collective-permute-start.6 = (f32[3,3,32,128]{3,2,1,0:T(8,128)}, f32[3,3,32,128]{3,2,1,0:T(8,128)S(1)}, u32[]{:S(2)}, u32[]{:S(2)}) collective-permute-start(f32[3,3,32,128]{3,2,1,0:T(8,128)} %get-tuple-element.31), channel_id=1, source_target_pairs={{8,0},{16,8},{24,16},{32,24},{40,32},{48,40},{56,48},{64,56},{72,6... | collective-permute-start | bytes 442376 | tf_op jit(solution)/shard_map/ppermute | solution.py:117
  68.4 18.9 %collective-permute-start.4 = (f32[3,72,128]{2,1,0:T(8,128)}, f32[3,72,128]{2,1,0:T(8,128)S(1)}, u32[]{:S(2)}, u32[]{:S(2)}) collective-permute-start(f32[3,72,128]{2,1,0:T(8,128)} %get-tuple-element.29), channel_id=1, source_target_pairs={{1,0},{2,1},{3,2},{4,3},{5,4},{6,5},{7,6},{9,8},{10,9},{11,10},{12... | collective-permute-start | bytes 331784 | tf_op jit(solution)/shard_map/ppermute | solution.py:115
  69.7 17.6 %collective-permute-start.5 = (f32[3,72,128]{2,1,0:T(8,128)}, f32[3,72,128]{2,1,0:T(8,128)S(1)}, u32[]{:S(2)}, u32[]{:S(2)}) collective-permute-start(f32[3,72,128]{2,1,0:T(8,128)} %get-tuple-element.30), channel_id=1, source_target_pairs={{0,1},{1,2},{2,3},{3,4},{4,5},{5,6},{6,7},{8,9},{9,10},{10,11},{11... | collective-permute-start | bytes 331784 | tf_op jit(solution)/shard_map/ppermute | solution.py:116
  79.0 17.9 %all-to-all-start.1 = ((f32[128,1,128]{2,1,0:T(1,128)}), f32[128,1,128]{2,1,0:T(1,128)S(1)}, u32[]{:S(2)}, u32[]{:S(2)}) async-start(f32[128,1,128]{2,1,0:T(1,128)} %bitcast.17), calls=%async_computation.1 | async-start | bytes 131072 | tf_op jit(solution)/shard_map/all_to_all | solution.py:463
  87.3 0.6 copy-start.5
  87.3 0.7 copy-start.6
  87.4 0.7 copy-start.3
  87.4 0.7 copy-start.4
